TPU v7x, 128 devices: a whole 4x4x4 slice. The times are simulated.
128 devices in a mesh: slab: 32 (over z, x, core), row: 4 (over y).
Axes of the slice: x: 4, y: 4, z: 4, core: 2. Of those that a mesh axis runs over, the one named last changes fastest.
Arguments:
- slot_brick: int32 [128, 128, 2], P(('slab', 'row')), may hold values from 0 to 255
- slot_count: int32 [128, 128, 2], P(('slab', 'row')), may hold values from 1 to 64, as said below
- point_cell: int32 [128, 128, 2, 64], P(('slab', 'row')), may hold values from 0 to 1023
- point_frac: float32 [128, 128, 2, 64], P(('slab', 'row')), may hold values from -0.5 to 0.5
- point_normal: float32 [128, 128, 2, 3, 64], P(('slab', 'row')), may hold values from -6 to 6
- point_weight: float32 [128, 128, 2, 64], P(('slab', 'row')), may hold values from 0.2 to 2
- guess: float32 [512, 64, 1024], P('slab', 'row'), may hold values from -4 to 4
Outputs:
- indicator: float32 [512, 64, 1024], P('slab', 'row')
Inputs may be any that keep to these rules, and one draw needn't show every extreme that they name: `slot_count`: every source block has at least one slot with exactly 64 live points.
All inputs are finite; a program needn't handle non-finite values.
Results may differ from a plain program's by a relative error of at most 0.0003.
Values sent between devices are 32-bit elements; how exact they have to be, the bound alone decides.
A program may use at most 64 MiB of HBM per device.

v0:
```python
import functools

import jax
import jax.numpy as jnp
from jax import lax
from jax.experimental import pallas as pl
from jax.experimental.pallas import tpu as pltpu
from jax.sharding import PartitionSpec as P

Z_DEV = 16
Y_DEV = 16
NX = 1024
CAP = 64
S_PEER = 2
SWEEPS = 3
HALF = Z_DEV // 2
TILE = (8, 128)
MESH = pl.DeviceIdType.MESH
F32 = jnp.float32
BF16 = jnp.bfloat16
I32 = jnp.int32


def iota(shape, dim):
    return lax.broadcasted_iota(I32, shape, dim)


def swap_halves(tiles):
    return pltpu.roll(tiles, 4, tiles.ndim - 2)


def low_half(shape):
    return iota(shape, len(shape) - 2) < 4


def neighbour(tiles, parity):
    shape = tiles.shape
    lane, sub = iota(shape, len(shape) - 1), iota(shape, len(shape) - 2) % 4
    if parity == 0:
        near = pltpu.roll(tiles, 1, len(shape) - 1)
        far = pltpu.roll(near, 1, len(shape) - 2)
        edge, end = lane == 0, sub == 0
    else:
        near = pltpu.roll(tiles, 127, len(shape) - 1)
        far = pltpu.roll(near, 7, len(shape) - 2)
        edge, end = lane == 127, sub == 3
    return jnp.where(edge, jnp.where(end, 0.0, far), near)


def by_rows(tiles, parity, function):
    pairs = tiles.reshape(tiles.shape[0] // 2, 2, *TILE)
    done = [function(pairs[:, q], (parity + q) % 2) for q in range(2)]
    return jnp.stack(done, axis=1).reshape(tiles.shape)


def parts(x):
    high = x.astype(BF16)
    return high, (x - high.astype(F32)).astype(BF16)


def pack_kernel(brick_ref, count_ref, cell_ref, frac_ref, normal_ref, weight_ref, out_ref):
    lane = iota((cell_ref.shape[0], CAP), 1)

    def rows(first, second):
        return jnp.concatenate([first, second], axis=1)

    live = rows(*[(lane < count_ref[:, s : s + 1]).astype(F32) for s in range(S_PEER)])
    out_ref[:, 0, :] = rows(cell_ref[:, 0, :], cell_ref[:, 1, :]).astype(F32)
    out_ref[:, 1, :] = rows(frac_ref[:, 0, :], frac_ref[:, 1, :])
    for ch in range(3):
        out_ref[:, 2 + ch, :] = rows(normal_ref[:, 0, ch, :], normal_ref[:, 1, ch, :]) * live
    out_ref[:, 5, :] = rows(weight_ref[:, 0, :], weight_ref[:, 1, :]) * live
    bricks = rows(*[jnp.broadcast_to(brick_ref[:, s : s + 1], lane.shape) for s in range(S_PEER)]).astype(F32)
    out_ref[:, 6, :] = bricks
    out_ref[:, 7, :] = bricks


def deinterleave(guess_ref, start_ref):
    col, row = iota((256, 256), 1), iota((256, 256), 0)
    place = (row == jnp.where(col < 128, 2 * col, 2 * col - 255)).astype(BF16)
    rows = Z_DEV * Y_DEV
    cells = iota((rows, 128), 0)
    even = (cells + cells // Y_DEV) % 2 == 0
    for i in range(4):
        chunk = guess_ref[:, :, 256 * i : 256 * (i + 1)].reshape(rows, 256)
        high, low = parts(chunk)
        split = jnp.dot(high, place, preferred_element_type=F32) + jnp.dot(low, place, preferred_element_type=F32)
        first, second = split[:, :128], split[:, 128:]
        colours = (jnp.where(even, first, second), jnp.where(even, second, first))
        for colour in range(2):
            for z in range(Z_DEV):
                base = ((colour * HALF + z % HALF) * Y_DEV) * 8 + (z // HALF) * 4 + i
                start_ref[pl.ds(base, Y_DEV, stride=8), :] = colours[colour][z * Y_DEV : (z + 1) * Y_DEV]


def splat_kernel(points_ref, guess_ref, rhs_ref, inv_ref, yface_ref, zface_ref, start_ref, acc, brick_v, brick_s, f1, f2, sem):
    sources = points_ref.shape[0] // 8
    brick_v[...] = points_ref[pl.ds(6, sources, stride=8), :].astype(I32)
    copy = pltpu.make_async_copy(brick_v, brick_s, sem)
    copy.start()

    def clear(b, _):
        acc[pl.ds(b * 8, 8)] = jnp.zeros((8, 32, 128), F32)
        return 0

    lax.fori_loop(0, Z_DEV * Y_DEV // 8, clear, 0)
    deinterleave(guess_ref, start_ref)
    copy.wait()

    lane = iota(TILE, 1)
    left = lane < CAP
    rank = iota(TILE, 0)
    wide_rank = iota((128, 128), 0)

    def group(g, _):
        cell, frac, n0, n1, n2, w, brick = [points_ref[pl.ds(g * 64 + r, 8, stride=8), :] for r in range(7)]
        cell, brick = cell.astype(I32), brick.astype(I32)
        parity, k = cell & 1, cell >> 1
        even = parity == 0
        wl = 0.5 * (0.5 - frac) * (0.5 - frac)
        wm = 0.75 - frac * frac
        wh = 0.5 * (0.5 + frac) * (0.5 + frac)
        beside = jnp.where(even, wh, wl)
        beyond = jnp.where(even, wl, wh)
        k2 = jnp.where(even, k - 1, k + 1)
        zl, yl = brick >> 4, brick & 15
        side = (parity + zl + yl + (zl >> 3)) & 1
        h1 = side * 4 + (k >> 7)
        h2 = (1 - side) * 4 + (k >> 7)
        inside = (k2 >= 0) & (k2 < NX // 2)
        h3 = jnp.where(inside, (1 - side) * 4 + (k2 >> 7), -1)
        none = jnp.full(TILE, -1, I32)
        zero = jnp.zeros(TILE, F32)

        def swap(x):
            return pltpu.roll(x, 64, 1)

        def both(x, y):
            return (jnp.where(left, x, swap(y)), jnp.where(left, swap(x), y))

        lanes_ = both(k & 127, k2 & 127)
        ha, hb = both(h1, h3), both(h2, none)
        wa, wb = both(wm, beyond), both(beside, zero)
        vals = [both(v, v) for v in (n0, n1, n2, w)]
        for r in range(8):
            for s in range(S_PEER):
                def row(x):
                    return x[s][r : r + 1, :]

                unit = jnp.where(rank == row(ha), row(wa), jnp.where(rank == row(hb), row(wb), 0.0))
                a = jnp.concatenate([unit * row(v) for v in vals], axis=0)
                onehot = (wide_rank == row(lanes_)).astype(F32).astype(BF16)
                out = lax.dot_general(
                    jnp.concatenate(parts(a), axis=0), onehot, (((1,), (1,)), ((), ())), preferred_element_type=F32
                )
                b = brick_s[g * 8 + r, s * CAP]
                acc[b] = acc[b] + (out[:32] + out[32:])
        return 0

    lax.fori_loop(0, sources // 8, group, 0)

    low = low_half((Y_DEV, *TILE))

    def fields(zp, ch):
        one = acc[pl.ds(zp * Y_DEV, Y_DEV), ch * 8 : ch * 8 + 8, :]
        two = acc[pl.ds((zp + HALF) * Y_DEV, Y_DEV), ch * 8 : ch * 8 + 8, :]
        return jnp.where(low, one, two), swap_halves(jnp.where(low, two, one))

    nil = jnp.zeros((1, *TILE), F32)
    for colour in range(2):
        for zp in range(HALF):
            f1[colour, zp, 0:1] = nil
            f1[colour, zp, Y_DEV + 1 : Y_DEV + 2] = nil

    def planes(pair, _):
        for odd in range(2):
            zp = pair * 2 + odd
            x = fields(zp, 0)
            y = fields(zp, 1)
            z = fields(zp, 2)
            d = fields(zp, 3)
            for colour in range(2):
                def slope(tiles, parity):
                    other = neighbour(tiles, parity)
                    return tiles - other if parity == 0 else other - tiles

                rhs_ref[colour, zp] = by_rows(x[1 - colour], (odd + colour) % 2, slope)
                f1[colour, zp, 1 : Y_DEV + 1] = y[colour]
                f2[colour, zp + 1] = z[colour]
                inv_ref[colour, zp] = 1.0 / (32.0 + 48.0 * d[colour])
                yface_ref[0, colour, zp] = y[colour][0]
                yface_ref[1, colour, zp] = y[colour][Y_DEV - 1]
        return 0

    lax.fori_loop(0, HALF // 2, planes, 0)
    zface_ref[0] = acc[0:Y_DEV, 16:24, :]
    zface_ref[1] = acc[(Z_DEV - 1) * Y_DEV :, 16:24, :]
    for colour in range(2):
        f2[colour, 0] = swap_halves(jnp.where(low, f2[colour, HALF], 0.0))
        f2[colour, HALF + 1] = swap_halves(jnp.where(low, 0.0, f2[colour, 1]))

    def finish(zp, _):
        for colour in range(2):
            o = 1 - colour
            spread = rhs_ref[colour, zp] + f1[o, zp, 2:] - f1[o, zp, :-2] + f2[o, zp + 2] - f2[o, zp]
            rhs_ref[colour, zp] = -6.0 * spread
        return 0

    lax.fori_loop(0, HALF, finish, 0)


def relax_kernel(rhs_in, inv_ref, start_ref, yface_ref, zface_ref, out_ref, v, zin, rhs, yin, zfin, send, recv, fsend, frecv):
    ns, nr = lax.axis_size("slab"), lax.axis_size("row")
    slab, line = lax.axis_index("slab"), lax.axis_index("row")
    last = Y_DEV + 1
    sides = [(1, 0), (-1, 0), (0, 1), (0, -1), (1, 1), (1, -1), (-1, 1), (-1, -1)]

    def exists(d):
        ok = True
        for step, at, size in ((d[0], slab, ns), (d[1], line, nr)):
            if step == 1:
                ok = (at < size - 1) if ok is True else ok & (at < size - 1)
            if step == -1:
                ok = (at > 0) if ok is True else ok & (at > 0)
        return ok

    def device(d):
        return (slab + d[0], line + d[1])

    nil = jnp.zeros((1, *TILE), F32)
    for n in range(7):
        for s in range(2):
            zin[n, s] = jnp.zeros((Y_DEV + 2, *TILE), F32)
        for zp in range(HALF):
            v[n, zp + 1, 0:1] = nil
            v[n, zp + 1, last:] = nil
    yin[...] = jnp.zeros(yin.shape, F32)
    zfin[...] = jnp.zeros(zfin.shape, F32)

    barrier = pltpu.get_barrier_semaphore()
    for d in sides:
        @pl.when(exists(d))
        def _():
            pl.semaphore_signal(barrier, inc=1, device_id=device(d), device_id_type=MESH)
    for colour in range(2):
        for zp in range(HALF):
            v[colour, zp + 1, 1:last] = start_ref[colour, zp]
    counts = [1 + (at > 0).astype(I32) + (at < size - 1).astype(I32) for at, size in ((slab, ns), (line, nr))]
    pl.semaphore_wait(barrier, counts[0] * counts[1] - 1)

    def copies(n):
        spans = {0: (pl.ds(1, Y_DEV), pl.ds(1, Y_DEV)), 1: (pl.ds(Y_DEV, 1), pl.ds(0, 1)), -1: (pl.ds(1, 1), pl.ds(last, 1))}
        for q, d in enumerate(sides):
            src_y, dst_y = spans[d[1]]
            if d[0] == 0:
                src, dst = v.at[n, pl.ds(1, HALF), src_y], v.at[n, pl.ds(1, HALF), dst_y]
            else:
                src, dst = v.at[n, HALF if d[0] == 1 else 1, src_y], zin.at[n, 0 if d[0] == 1 else 1, dst_y]
            yield d, pltpu.make_async_remote_copy(src, dst, send.at[n, q], recv.at[n, q], device(d), MESH)

    def face_copies():
        for q, d in enumerate(sides[:4]):
            s = 0 if d[q // 2] == 1 else 1
            if d[0] == 0:
                src, dst = yface_ref.at[1 - s], yin.at[s]
            else:
                src, dst = zface_ref.at[1 - s], zfin.at[s]
            yield d, pltpu.make_async_remote_copy(src, dst, fsend.at[q], frecv.at[q], device(d), MESH)

    def start_all(pairs):
        for d, copy in pairs:
            @pl.when(exists(d))
            def _():
                copy.start()

    def take_all(pairs):
        for d, copy in pairs:
            @pl.when(exists((-d[0], -d[1])))
            def _():
                copy.wait_recv()

    def sent_all(pairs):
        for d, copy in pairs:
            @pl.when(exists(d))
            def _():
                copy.wait_send()

    def rims(n):
        low = low_half((Y_DEV + 2, *TILE))
        v[n, 0] = swap_halves(jnp.where(low, v[n, HALF], zin[n, 0]))
        v[n, HALF + 1] = swap_halves(jnp.where(low, zin[n, 1], v[n, 1]))

    start_all(face_copies())
    start_all(copies(0))
    start_all(copies(1))
    take_all(face_copies())
    low = low_half((Y_DEV, *TILE))
    for colour in range(2):
        for zp in range(HALF):
            rhs[colour, zp] = rhs_in[colour, zp]
        for zp in range(HALF):
            rhs[colour, zp, 0] += 6.0 * yin[0, 1 - colour, zp]
            rhs[colour, zp, Y_DEV - 1] -= 6.0 * yin[1, 1 - colour, zp]
        below, above = zfin[0], zfin[1]
        if colour == 1:
            below, above = swap_halves(below), swap_halves(above)
        rhs[colour, 0] += jnp.where(low, 6.0 * below, 0.0)
        rhs[colour, HALF - 1] -= jnp.where(low, 0.0, 6.0 * above)
    for n in range(2):
        take_all(copies(n))
        rims(n)

    for step in range(2 * SWEEPS):
        same, opp, new, colour = step, step + 1, step + 2, step % 2

        def planes(pair, _):
            for odd in range(2):
                zp = pair * 2 + odd
                s1 = v[same, zp] + v[same, zp + 2]
                o1 = v[opp, zp] + v[opp, zp + 2]
                s0 = v[same, zp + 1]
                faces = s1[1:last] + s0[:-2] + s0[2:]
                diagonal = s1[:-2] + s1[2:]
                across = 2.0 * faces + (o1[:-2] + o1[2:])
                total = rhs[colour, zp] + 2.0 * diagonal + across
                value = (total + by_rows(across, (odd + colour) % 2, neighbour)) * inv_ref[colour, zp]
                if step < 2 * SWEEPS - 1:
                    v[new, zp + 1, 1:last] = value
                if step == 2 * SWEEPS - 2:
                    out_ref[0, zp] = value
                if step == 2 * SWEEPS - 1:
                    out_ref[1, zp] = value
            return 0

        lax.fori_loop(0, HALF // 2, planes, 0)
        if step < 2 * SWEEPS - 1:
            start_all(copies(new))
            take_all(copies(new))
            rims(new)

    sent_all(face_copies())
    for n in range(2 * SWEEPS + 1):
        sent_all(copies(n))


def interleave_kernel(in_ref, out_ref):
    col, row = iota((256, 256), 1), iota((256, 256), 0)
    place = (col == jnp.where(row < 128, 2 * row, 2 * row - 255)).astype(BF16)
    rows = Z_DEV * Y_DEV
    cells = iota((rows, 128), 0)
    even = (cells + cells // Y_DEV) % 2 == 0
    for i in range(4):
        colours = []
        for colour in range(2):
            base = [((colour * HALF + z % HALF) * Y_DEV) * 8 + (z // HALF) * 4 + i for z in range(Z_DEV)]
            colours.append(jnp.concatenate([in_ref[pl.ds(b, Y_DEV, stride=8), :] for b in base], axis=0))
        red, black = colours
        both = jnp.concatenate([jnp.where(even, red, black), jnp.where(even, black, red)], axis=1)
        high, low = parts(both)
        merged = jnp.dot(high, place, preferred_element_type=F32) + jnp.dot(low, place, preferred_element_type=F32)
        out_ref[:, :, 256 * i : 256 * (i + 1)] = merged.reshape(Z_DEV, Y_DEV, 256)


VM = pl.BlockSpec(memory_space=pltpu.VMEM)


def call(kernel, outs, scratch, count, limit, **params):
    return pl.pallas_call(
        kernel,
        out_shape=outs,
        in_specs=[VM] * count,
        out_specs=jax.tree.map(lambda _: VM, outs),
        scratch_shapes=scratch,
        compiler_params=pltpu.CompilerParams(vmem_limit_bytes=limit << 20, **params),
    )


def shards(slot_brick, slot_count, point_cell, point_frac, point_normal, point_weight, guess):
    peers = point_cell.shape[1]
    full = jax.ShapeDtypeStruct((2, HALF, Y_DEV, *TILE), F32)
    sent = call(pack_kernel, jax.ShapeDtypeStruct((peers, 8, 128), F32), [], 6, 16)(
        slot_brick[0], slot_count[0], point_cell[0], point_frac[0], point_normal[0], point_weight[0]
    )
    points = lax.all_to_all(sent, ("slab", "row"), split_axis=0, concat_axis=0, tiled=True)
    outs = (
        full,
        full,
        jax.ShapeDtypeStruct((2, 2, HALF, *TILE), F32),
        jax.ShapeDtypeStruct((2, Y_DEV, *TILE), F32),
        jax.ShapeDtypeStruct((2 * HALF * Y_DEV * 8, 128), F32),
    )
    rhs, inv, yface, zface, start = call(
        splat_kernel,
        outs,
        [
            pltpu.VMEM((Z_DEV * Y_DEV, 32, 128), F32),
            pltpu.VMEM((peers, 128), I32),
            pltpu.SMEM((peers, 128), I32),
            pltpu.VMEM((2, HALF, Y_DEV + 2, *TILE), F32),
            pltpu.VMEM((2, HALF + 2, Y_DEV, *TILE), F32),
            pltpu.SemaphoreType.DMA,
        ],
        2,
        32,
    )(points.reshape(peers * 8, 128), guess)
    relaxed = call(
        relax_kernel,
        full,
        [
            pltpu.VMEM((7, HALF + 2, Y_DEV + 2, *TILE), F32),
            pltpu.VMEM((7, 2, Y_DEV + 2, *TILE), F32),
            pltpu.VMEM((2, HALF, Y_DEV, *TILE), F32),
            pltpu.VMEM((2, 2, HALF, *TILE), F32),
            pltpu.VMEM((2, Y_DEV, *TILE), F32),
            pltpu.SemaphoreType.DMA((7, 8)),
            pltpu.SemaphoreType.DMA((7, 8)),
            pltpu.SemaphoreType.DMA((4,)),
            pltpu.SemaphoreType.DMA((4,)),
        ],
        5,
        32,
        collective_id=0,
        has_side_effects=True,
    )(rhs, inv, start.reshape(full.shape), yface, zface)
    return call(interleave_kernel, jax.ShapeDtypeStruct((Z_DEV, Y_DEV, NX), F32), [], 1, 16)(relaxed.reshape(-1, 128))


def solution(mesh):
    placed = (
        P(("slab", "row"), None, None),
        P(("slab", "row"), None, None),
        P(("slab", "row"), None, None, None),
        P(("slab", "row"), None, None, None),
        P(("slab", "row"), None, None, None, None),
        P(("slab", "row"), None, None, None),
        P("slab", "row", None),
    )
    return jax.shard_map(
        shards, mesh=mesh, in_specs=placed, out_specs=P("slab", "row", None), check_vma=False
    )
```

profile of v0, /device:TPU:7, one launch (start us, length us, event | category | flops | bytes accessed | tf_op | source)
XLA Modules:
  0.0 73.6 jit_solution(1767730642540238945)
XLA Ops:
  0.0 0.0 copy-start.5
  0.0 0.0 copy-start.2
  0.0 0.8 %copy.8 = s32[1,128,2]{2,1,0:T(8,128)S(1)} copy(s32[1,128,2]{1,2,0:T(2,128)} %param.7) | data formatting | bytes 2048 | tf_op args[0]
  0.8 0.0 copy-done.5
  0.8 0.1 copy.9
  0.9 0.0 copy-done.2
  0.9 0.0 copy-start.3
  1.0 0.0 copy-start.4
  1.0 0.1 copy.10
  1.1 0.7 copy-done.3
  1.8 0.0 copy-start.1
  1.8 0.1 copy.11
  1.9 0.0 copy-done.4
  1.9 0.1 copy.13
  2.0 0.7 copy-done.1
  2.7 0.3 copy.12
  3.0 0.0 copy-start
  3.0 0.7 shard_map.73
  3.7 22.7 %all_to_all.5 = f32[128,8,128]{2,1,0:T(8,128)S(1)} all-to-all(f32[128,8,128]{2,1,0:T(8,128)S(1)} %shard_map.73), channel_id=1, replica_groups=mesh['slab'=32,'row'=4] {'slab','row'}, dimensions={0} | all-to-all | bytes 1048576 | tf_op jit(solution)/shard_map/all_to_all | solution.py:384
  26.4 0.0 copy-done
  26.4 11.0 %shard_map.74 = (f32[2,8,16,8,128]{4,3,2,1,0:T(8,128)S(1)}, f32[2,8,16,8,128]{4,3,2,1,0:T(8,128)S(1)}, f32[2,2,8,8,128]{4,3,2,1,0:T(8,128)S(1)}, f32[2,16,8,128]{3,2,1,0:T(8,128)S(1)}, f32[2048,128]{1,0:T(8,128)S(1)}) custom-call(f32[1024,128]{1,0:T(8,128)S(1)} %bitcast.10, f32[16,16,1024]{2,1,0:T(8,128)S(1)} %copy-done), custom_call_target="tpu_custom_call" | custom-call | tf_op jit(solution)/shard_map/pallas_call | solution.py:392
  37.4 34.6 %shard_map.75 = f32[2,8,16,8,128]{4,3,2,1,0:T(8,128)S(1)} custom-call(f32[2,8,16,8,128]{4,3,2,1,0:T(8,128)S(1)} %get-tuple-element.10.rhs_in, f32[2,8,16,8,128]{4,3,2,1,0:T(8,128)S(1)} %get-tuple-element.11.inv_ref, f32[2,8,16,8,128]{4,3,2,1,0:T(8,128)S(1)} %bitcast.12, f32[2,2,8,8,128]{4,3,2,1,0:T(8,128)S(1)} %get-tuple-element.13.yface_ref, ...), custom_call_target="tpu_custom_call" | custom-call | tf_op jit(solution)/shard_map/pallas_call | solution.py:406
  72.1 1.5 %shard_map.76 = f32[16,16,1024]{2,1,0:T(8,128)} custom-call(f32[2048,128]{1,0:T(8,128)S(1)} %bitcast.9), custom_call_target="tpu_custom_call" | custom-call | tf_op jit(solution)/shard_map/pallas_call | solution.py:425
Async XLA Ops:
  0.0 0.8 %copy-start.5 = (s32[1,128,2]{1,2,0:T(2,128)S(1)}, s32[1,128,2]{1,2,0:T(2,128)}, u32[]{:S(2)}) copy-start(s32[1,128,2]{1,2,0:T(2,128)} %param.8) | copy-start | bytes 3076
  0.0 0.9 %copy-start.2 = (s32[1,128,2,64]{1,3,2,0:T(8,128)S(1)}, s32[1,128,2,64]{1,3,2,0:T(8,128)}, u32[]{:S(2)}) copy-start(s32[1,128,2,64]{1,3,2,0:T(8,128)} %param.9) | copy-start | bytes 196612
  0.9 0.8 %copy-start.3 = (f32[1,128,2,64]{1,3,2,0:T(8,128)S(1)}, f32[1,128,2,64]{1,3,2,0:T(8,128)}, u32[]{:S(2)}) copy-start(f32[1,128,2,64]{1,3,2,0:T(8,128)} %param.10) | copy-start | bytes 196612
  1.0 0.9 %copy-start.4 = (f32[1,128,2,64]{1,3,2,0:T(8,128)S(1)}, f32[1,128,2,64]{1,3,2,0:T(8,128)}, u32[]{:S(2)}) copy-start(f32[1,128,2,64]{1,3,2,0:T(8,128)} %param.12) | copy-start | bytes 196612
  1.8 0.9 %copy-start.1 = (f32[1,128,2,3,64]{1,4,3,2,0:T(8,128)S(1)}, f32[1,128,2,3,64]{1,4,3,2,0:T(8,128)}, u32[]{:S(2)}) copy-start(f32[1,128,2,3,64]{1,4,3,2,0:T(8,128)} %param.11) | copy-start | bytes 589828
  3.0 23.4 %copy-start = (f32[16,16,1024]{2,1,0:T(8,128)S(1)}, f32[16,16,1024]{2,1,0:T(8,128)}, u32[]{:S(2)}) copy-start(f32[16,16,1024]{2,1,0:T(8,128)} %guess_ref.1) | copy-start | bytes 3145732
where the time goes:
time: 73.8 us; the launch traced here: 73.6 us
  Pallas kernels  47.8 us (65%)
  blocking collectives  22.7 us (31%)
  local copies, waits for them, and re-layouts  2.94 us (4%)
    pallas_call x1, Pallas kernels, shards(): call(relax_kernel, full, [pltpu.VMEM((7, HALF + 2, Y_DEV + 2, *TILE), F32...  34.6 us
    all_to_all x1, blocking collectives, shards(): lax.all_to_all(sent, ('slab', 'row'), split_axis=0, concat_axis=0, tiled=...  22.7 us
    pallas_call x1, Pallas kernels, shards(): call(splat_kernel, outs, [pltpu.VMEM((Z_DEV * Y_DEV, 32, 128), F32), pltp...  11 us
    unnamed x18, local copies, waits for them, and re-layouts  2.94 us
    pallas_call x1, Pallas kernels, shards(): call(interleave_kernel, jax.ShapeDtypeStruct((Z_DEV, Y_DEV, NX), F32), []...  1.49 us

commit v1 on v0

--- a/solution.py
+++ b/solution.py
@@ -56,23 +56,6 @@
 def parts(x):
     high = x.astype(BF16)
     return high, (x - high.astype(F32)).astype(BF16)
-
-
-def pack_kernel(brick_ref, count_ref, cell_ref, frac_ref, normal_ref, weight_ref, out_ref):
-    lane = iota((cell_ref.shape[0], CAP), 1)
-
-    def rows(first, second):
-        return jnp.concatenate([first, second], axis=1)
-
-    live = rows(*[(lane < count_ref[:, s : s + 1]).astype(F32) for s in range(S_PEER)])
-    out_ref[:, 0, :] = rows(cell_ref[:, 0, :], cell_ref[:, 1, :]).astype(F32)
-    out_ref[:, 1, :] = rows(frac_ref[:, 0, :], frac_ref[:, 1, :])
-    for ch in range(3):
-        out_ref[:, 2 + ch, :] = rows(normal_ref[:, 0, ch, :], normal_ref[:, 1, ch, :]) * live
-    out_ref[:, 5, :] = rows(weight_ref[:, 0, :], weight_ref[:, 1, :]) * live
-    bricks = rows(*[jnp.broadcast_to(brick_ref[:, s : s + 1], lane.shape) for s in range(S_PEER)]).astype(F32)
-    out_ref[:, 6, :] = bricks
-    out_ref[:, 7, :] = bricks
 
 
 def deinterleave(guess_ref, start_ref):
@@ -93,7 +76,158 @@
                 start_ref[pl.ds(base, Y_DEV, stride=8), :] = colours[colour][z * Y_DEV : (z + 1) * Y_DEV]
 
 
-def splat_kernel(points_ref, guess_ref, rhs_ref, inv_ref, yface_ref, zface_ref, start_ref, acc, brick_v, brick_s, f1, f2, sem):
+SIDES = [(0, 1), (0, -1), (1, 0), (-1, 0), (1, 1), (1, -1), (-1, 1), (-1, -1)]
+LAST = Y_DEV + 1
+RIM = (HALF + 2, Y_DEV + 2, *TILE)
+
+
+class Grid:
+    def __init__(self):
+        self.ns, self.nr = lax.axis_size("slab"), lax.axis_size("row")
+        self.slab, self.line = lax.axis_index("slab"), lax.axis_index("row")
+
+    def exists(self, d):
+        tests = []
+        for step, at, size in ((d[0], self.slab, self.ns), (d[1], self.line, self.nr)):
+            if step == 1:
+                tests.append(at < size - 1)
+            if step == -1:
+                tests.append(at > 0)
+        return tests[0] if len(tests) == 1 else tests[0] & tests[1]
+
+    def device(self, d):
+        return (self.slab + d[0], self.line + d[1])
+
+    def greet_neighbours(self):
+        barrier = pltpu.get_barrier_semaphore()
+        for d in SIDES:
+            @pl.when(self.exists(d))
+            def _():
+                pl.semaphore_signal(barrier, inc=1, device_id=self.device(d), device_id_type=MESH)
+
+    def await_neighbours(self):
+        counts = [
+            1 + (at > 0).astype(I32) + (at < size - 1).astype(I32)
+            for at, size in ((self.slab, self.ns), (self.line, self.nr))
+        ]
+        pl.semaphore_wait(pltpu.get_barrier_semaphore(), counts[0] * counts[1] - 1)
+
+    def start(self, pairs):
+        for d, copy in pairs:
+            @pl.when(self.exists(d))
+            def _():
+                copy.start()
+
+    def take(self, pairs):
+        for d, copy in pairs:
+            @pl.when(self.exists((-d[0], -d[1])))
+            def _():
+                copy.wait_recv()
+
+    def sent(self, pairs):
+        for d, copy in pairs:
+            @pl.when(self.exists(d))
+            def _():
+                copy.wait_send()
+
+    def clear_outside(self, tiles, edge):
+        for d in SIDES:
+            @pl.when(jnp.logical_not(self.exists((-d[0], -d[1]))))
+            def _():
+                if d[0] == 0:
+                    y = 0 if d[1] == 1 else LAST
+                    tiles[1 : HALF + 1, y : y + 1] = jnp.zeros((HALF, 1, *TILE), F32)
+                else:
+                    at, size = {0: (1, Y_DEV), 1: (0, 1), -1: (LAST, 1)}[d[1]]
+                    edge[0 if d[0] == 1 else 1, at : at + size] = jnp.zeros((size, *TILE), F32)
+
+    def halo(self, tiles, edge, send, recv):
+        spans = {0: (pl.ds(1, Y_DEV), pl.ds(1, Y_DEV)), 1: (pl.ds(Y_DEV, 1), pl.ds(0, 1)), -1: (pl.ds(1, 1), pl.ds(LAST, 1))}
+        pairs = []
+        for q, d in enumerate(SIDES):
+            src_y, dst_y = spans[d[1]]
+            if d[0] == 0:
+                src, dst = tiles.at[pl.ds(1, HALF), src_y], tiles.at[pl.ds(1, HALF), dst_y]
+            else:
+                src, dst = tiles.at[HALF if d[0] == 1 else 1, src_y], edge.at[0 if d[0] == 1 else 1, dst_y]
+            pairs.append((d, pltpu.make_async_remote_copy(src, dst, send.at[q], recv.at[q], self.device(d), MESH)))
+        return pairs
+
+
+def rims(tiles, edge):
+    low = low_half((Y_DEV + 2, *TILE))
+    tiles[0] = swap_halves(jnp.where(low, tiles[HALF], edge[0]))
+    tiles[HALF + 1] = swap_halves(jnp.where(low, edge[1], tiles[1]))
+
+
+def bin_kernel(
+    brick_ref, count_ref, cell_ref, frac_ref, normal_ref, weight_ref, guess_ref, points_ref, v_ref,
+    packed, split, edge, psend, precv, send, recv,
+):
+    grid = Grid()
+    peers = grid.ns * grid.nr
+    me = grid.slab * grid.nr + grid.line
+    barrier = pltpu.get_barrier_semaphore()
+    for colour in range(2):
+        grid.clear_outside(v_ref.at[colour], edge.at[colour])
+
+    def peer(i):
+        t = lax.rem(me + i, peers)
+        return t, (t // grid.nr, lax.rem(t, grid.nr))
+
+    def greet(i, _):
+        pl.semaphore_signal(barrier, inc=1, device_id=peer(i)[1], device_id_type=MESH)
+        return 0
+
+    lax.fori_loop(1, peers, greet, 0)
+
+    point = iota((CAP, peers), 0)
+    live = jnp.concatenate([(point < count_ref[s : s + 1, :]).astype(F32) for s in range(S_PEER)], axis=0)
+
+    def put(r, first, second, mask=None):
+        rows = jnp.concatenate([first, second], axis=0).astype(F32)
+        packed[pl.ds(r, peers, stride=8), :] = (rows if mask is None else rows * mask).T
+
+    put(0, cell_ref[0], cell_ref[1])
+    put(1, frac_ref[0], frac_ref[1])
+    for ch in range(3):
+        put(2 + ch, normal_ref[0, ch], normal_ref[1, ch], live)
+    put(5, weight_ref[0], weight_ref[1], live)
+    put(6, *[jnp.broadcast_to(brick_ref[s : s + 1, :], point.shape) for s in range(S_PEER)])
+    packed[pl.ds(7, peers, stride=8), :] = jnp.zeros((peers, 128), F32)
+
+    def tile(t):
+        return pl.ds(pl.multiple_of(t * 8, 8), 8)
+
+    pl.semaphore_wait(barrier, peers - 1)
+
+    def send_points(i, _):
+        t, device = peer(i)
+        pltpu.make_async_remote_copy(packed.at[tile(t)], points_ref.at[tile(me)], psend, precv, device, MESH).start()
+        return 0
+
+    lax.fori_loop(1, peers, send_points, 0)
+    points_ref[tile(me), :] = packed[tile(me), :]
+    deinterleave(guess_ref, split)
+    for colour in range(2):
+        for zp in range(HALF):
+            at = (colour * HALF + zp) * Y_DEV * 8
+            v_ref[colour, zp + 1, 1:LAST] = split[at : at + Y_DEV * 8, :].reshape(Y_DEV, *TILE)
+    halos = [grid.halo(v_ref.at[c], edge.at[c], send.at[c], recv.at[c]) for c in range(2)]
+    for colour in range(2):
+        grid.start(halos[colour])
+    for colour in range(2):
+        grid.take(halos[colour])
+        rims(v_ref.at[colour], edge.at[colour])
+    others = pl.ds(0, (peers - 1) * 8)
+    every = pltpu.make_async_remote_copy(packed.at[others], points_ref.at[others], psend, precv, peer(1)[1], MESH)
+    every.wait_recv()
+    every.wait_send()
+    for colour in range(2):
+        grid.sent(halos[colour])
+
+
+def splat_kernel(points_ref, rhs_ref, inv_ref, yface_ref, zface_ref, acc, brick_v, brick_s, f1, f2, sem):
     sources = points_ref.shape[0] // 8
     brick_v[...] = points_ref[pl.ds(6, sources, stride=8), :].astype(I32)
     copy = pltpu.make_async_copy(brick_v, brick_s, sem)
@@ -104,7 +238,6 @@
         return 0
 
     lax.fori_loop(0, Z_DEV * Y_DEV // 8, clear, 0)
-    deinterleave(guess_ref, start_ref)
     copy.wait()
 
     lane = iota(TILE, 1)
@@ -209,95 +342,40 @@
     lax.fori_loop(0, HALF, finish, 0)
 
 
-def relax_kernel(rhs_in, inv_ref, start_ref, yface_ref, zface_ref, out_ref, v, zin, rhs, yin, zfin, send, recv, fsend, frecv):
-    ns, nr = lax.axis_size("slab"), lax.axis_size("row")
-    slab, line = lax.axis_index("slab"), lax.axis_index("row")
-    last = Y_DEV + 1
-    sides = [(1, 0), (-1, 0), (0, 1), (0, -1), (1, 1), (1, -1), (-1, 1), (-1, -1)]
-
-    def exists(d):
-        ok = True
-        for step, at, size in ((d[0], slab, ns), (d[1], line, nr)):
-            if step == 1:
-                ok = (at < size - 1) if ok is True else ok & (at < size - 1)
-            if step == -1:
-                ok = (at > 0) if ok is True else ok & (at > 0)
-        return ok
-
-    def device(d):
-        return (slab + d[0], line + d[1])
-
-    nil = jnp.zeros((1, *TILE), F32)
-    for n in range(7):
-        for s in range(2):
-            zin[n, s] = jnp.zeros((Y_DEV + 2, *TILE), F32)
-        for zp in range(HALF):
-            v[n, zp + 1, 0:1] = nil
-            v[n, zp + 1, last:] = nil
-    yin[...] = jnp.zeros(yin.shape, F32)
-    zfin[...] = jnp.zeros(zfin.shape, F32)
-
-    barrier = pltpu.get_barrier_semaphore()
-    for d in sides:
-        @pl.when(exists(d))
+def relax_kernel(rhs_in, inv_ref, start_ref, yface_ref, zface_ref, out_ref, v, edge, rhs, yin, zfin, send, recv, fsend, frecv):
+    grid = Grid()
+    versions = [start_ref.at[0], start_ref.at[1]] + [v.at[n] for n in range(2 * SWEEPS - 1)]
+
+    def clear(n, _):
+        grid.clear_outside(v.at[n], edge.at[n])
+        return 0
+
+    lax.fori_loop(0, 2 * SWEEPS - 1, clear, 0)
+    for q, d in enumerate(SIDES[:4]):
+        s = 0 if d[q < 2] == 1 else 1
+        @pl.when(jnp.logical_not(grid.exists((-d[0], -d[1]))))
         def _():
-            pl.semaphore_signal(barrier, inc=1, device_id=device(d), device_id_type=MESH)
-    for colour in range(2):
-        for zp in range(HALF):
-            v[colour, zp + 1, 1:last] = start_ref[colour, zp]
-    counts = [1 + (at > 0).astype(I32) + (at < size - 1).astype(I32) for at, size in ((slab, ns), (line, nr))]
-    pl.semaphore_wait(barrier, counts[0] * counts[1] - 1)
-
-    def copies(n):
-        spans = {0: (pl.ds(1, Y_DEV), pl.ds(1, Y_DEV)), 1: (pl.ds(Y_DEV, 1), pl.ds(0, 1)), -1: (pl.ds(1, 1), pl.ds(last, 1))}
-        for q, d in enumerate(sides):
-            src_y, dst_y = spans[d[1]]
             if d[0] == 0:
-                src, dst = v.at[n, pl.ds(1, HALF), src_y], v.at[n, pl.ds(1, HALF), dst_y]
+                yin[s] = jnp.zeros(yin.shape[1:], F32)
             else:
-                src, dst = v.at[n, HALF if d[0] == 1 else 1, src_y], zin.at[n, 0 if d[0] == 1 else 1, dst_y]
-            yield d, pltpu.make_async_remote_copy(src, dst, send.at[n, q], recv.at[n, q], device(d), MESH)
-
-    def face_copies():
-        for q, d in enumerate(sides[:4]):
-            s = 0 if d[q // 2] == 1 else 1
-            if d[0] == 0:
-                src, dst = yface_ref.at[1 - s], yin.at[s]
-            else:
-                src, dst = zface_ref.at[1 - s], zfin.at[s]
-            yield d, pltpu.make_async_remote_copy(src, dst, fsend.at[q], frecv.at[q], device(d), MESH)
-
-    def start_all(pairs):
-        for d, copy in pairs:
-            @pl.when(exists(d))
-            def _():
-                copy.start()
-
-    def take_all(pairs):
-        for d, copy in pairs:
-            @pl.when(exists((-d[0], -d[1])))
-            def _():
-                copy.wait_recv()
-
-    def sent_all(pairs):
-        for d, copy in pairs:
-            @pl.when(exists(d))
-            def _():
-                copy.wait_send()
-
-    def rims(n):
-        low = low_half((Y_DEV + 2, *TILE))
-        v[n, 0] = swap_halves(jnp.where(low, v[n, HALF], zin[n, 0]))
-        v[n, HALF + 1] = swap_halves(jnp.where(low, zin[n, 1], v[n, 1]))
-
-    start_all(face_copies())
-    start_all(copies(0))
-    start_all(copies(1))
-    take_all(face_copies())
-    low = low_half((Y_DEV, *TILE))
+                zfin[s] = jnp.zeros(zfin.shape[1:], F32)
+    grid.greet_neighbours()
+    grid.await_neighbours()
+    faces = []
+    for q, d in enumerate(SIDES[:4]):
+        s = 0 if d[q < 2] == 1 else 1
+        if d[0] == 0:
+            src, dst = yface_ref.at[1 - s], yin.at[s]
+        else:
+            src, dst = zface_ref.at[1 - s], zfin.at[s]
+        faces.append((d, pltpu.make_async_remote_copy(src, dst, fsend.at[q], frecv.at[q], grid.device(d), MESH)))
+    grid.start(faces)
     for colour in range(2):
         for zp in range(HALF):
             rhs[colour, zp] = rhs_in[colour, zp]
+    low = low_half((Y_DEV, *TILE))
+    grid.take(faces)
+    for colour in range(2):
         for zp in range(HALF):
             rhs[colour, zp, 0] += 6.0 * yin[0, 1 - colour, zp]
             rhs[colour, zp, Y_DEV - 1] -= 6.0 * yin[1, 1 - colour, zp]
@@ -306,41 +384,51 @@
             below, above = swap_halves(below), swap_halves(above)
         rhs[colour, 0] += jnp.where(low, 6.0 * below, 0.0)
         rhs[colour, HALF - 1] -= jnp.where(low, 0.0, 6.0 * above)
-    for n in range(2):
-        take_all(copies(n))
-        rims(n)
-
+
+    sent = [faces]
     for step in range(2 * SWEEPS):
-        same, opp, new, colour = step, step + 1, step + 2, step % 2
-
-        def planes(pair, _):
+        same, opp, colour = versions[step], versions[step + 1], step % 2
+        new = versions[step + 2] if step < 2 * SWEEPS - 1 else None
+
+        def update(zp, y, count):
+            parity = (zp if isinstance(zp, int) else zp[1]) + y + colour
+            zp = zp if isinstance(zp, int) else zp[0]
+            s1 = same[zp, y : y + count + 2] + same[zp + 2, y : y + count + 2]
+            o1 = opp[zp, y : y + count + 2] + opp[zp + 2, y : y + count + 2]
+            s0 = same[zp + 1, y : y + count + 2]
+            around = s1[1:-1] + s0[:-2] + s0[2:]
+            diagonal = s1[:-2] + s1[2:]
+            across = 2.0 * around + (o1[:-2] + o1[2:])
+            total = rhs[colour, zp, y : y + count] + 2.0 * diagonal + across
+            other = neighbour(across, parity % 2) if count == 1 else by_rows(across, parity % 2, neighbour)
+            value = (total + other) * inv_ref[colour, zp, y : y + count]
+            if new is not None:
+                new[zp + 1, y + 1 : y + 1 + count] = value
+            if step >= 2 * SWEEPS - 2:
+                out_ref[colour, zp, y : y + count] = value
+
+        for zp in range(1, HALF - 1):
+            for y in (0, Y_DEV - 1):
+                update(zp, y, 1)
+        for zp in (0, HALF - 1):
+            update(zp, 0, Y_DEV)
+        if new is not None:
+            pairs = grid.halo(new, edge.at[step], send.at[step], recv.at[step])
+            grid.start(pairs)
+            sent.append(pairs)
+
+        def inner(pair, _):
             for odd in range(2):
-                zp = pair * 2 + odd
-                s1 = v[same, zp] + v[same, zp + 2]
-                o1 = v[opp, zp] + v[opp, zp + 2]
-                s0 = v[same, zp + 1]
-                faces = s1[1:last] + s0[:-2] + s0[2:]
-                diagonal = s1[:-2] + s1[2:]
-                across = 2.0 * faces + (o1[:-2] + o1[2:])
-                total = rhs[colour, zp] + 2.0 * diagonal + across
-                value = (total + by_rows(across, (odd + colour) % 2, neighbour)) * inv_ref[colour, zp]
-                if step < 2 * SWEEPS - 1:
-                    v[new, zp + 1, 1:last] = value
-                if step == 2 * SWEEPS - 2:
-                    out_ref[0, zp] = value
-                if step == 2 * SWEEPS - 1:
-                    out_ref[1, zp] = value
+                update((pair * 2 + 1 + odd, 1 + odd), 1, Y_DEV - 2)
             return 0
 
-        lax.fori_loop(0, HALF // 2, planes, 0)
-        if step < 2 * SWEEPS - 1:
-            start_all(copies(new))
-            take_all(copies(new))
-            rims(new)
-
-    sent_all(face_copies())
-    for n in range(2 * SWEEPS + 1):
-        sent_all(copies(n))
+        lax.fori_loop(0, HALF // 2 - 1, inner, 0)
+        if new is not None:
+            grid.take(pairs)
+            rims(new, edge.at[step])
+
+    for pairs in sent:
+        grid.sent(pairs)
 
 
 def interleave_kernel(in_ref, out_ref):
@@ -378,18 +466,35 @@
 def shards(slot_brick, slot_count, point_cell, point_frac, point_normal, point_weight, guess):
     peers = point_cell.shape[1]
     full = jax.ShapeDtypeStruct((2, HALF, Y_DEV, *TILE), F32)
-    sent = call(pack_kernel, jax.ShapeDtypeStruct((peers, 8, 128), F32), [], 6, 16)(
-        slot_brick[0], slot_count[0], point_cell[0], point_frac[0], point_normal[0], point_weight[0]
-    )
-    points = lax.all_to_all(sent, ("slab", "row"), split_axis=0, concat_axis=0, tiled=True)
+    steps = 2 * SWEEPS - 1
+
+    def last(x):
+        return jnp.moveaxis(x[0], 0, -1)
+
+    points, start = call(
+        bin_kernel,
+        (jax.ShapeDtypeStruct((peers * 8, 128), F32), jax.ShapeDtypeStruct((2, *RIM), F32)),
+        [
+            pltpu.VMEM((peers * 8, 128), F32),
+            pltpu.VMEM((2 * HALF * Y_DEV * 8, 128), F32),
+            pltpu.VMEM((2, 2, Y_DEV + 2, *TILE), F32),
+            pltpu.SemaphoreType.DMA,
+            pltpu.SemaphoreType.DMA,
+            pltpu.SemaphoreType.DMA((2, 8)),
+            pltpu.SemaphoreType.DMA((2, 8)),
+        ],
+        7,
+        24,
+        collective_id=0,
+        has_side_effects=True,
+    )(last(slot_brick), last(slot_count), last(point_cell), last(point_frac), last(point_normal), last(point_weight), guess)
     outs = (
         full,
         full,
         jax.ShapeDtypeStruct((2, 2, HALF, *TILE), F32),
         jax.ShapeDtypeStruct((2, Y_DEV, *TILE), F32),
-        jax.ShapeDtypeStruct((2 * HALF * Y_DEV * 8, 128), F32),
     )
-    rhs, inv, yface, zface, start = call(
+    rhs, inv, yface, zface = call(
         splat_kernel,
         outs,
         [
@@ -400,28 +505,28 @@
             pltpu.VMEM((2, HALF + 2, Y_DEV, *TILE), F32),
             pltpu.SemaphoreType.DMA,
         ],
-        2,
+        1,
         32,
-    )(points.reshape(peers * 8, 128), guess)
+    )(points)
     relaxed = call(
         relax_kernel,
         full,
         [
-            pltpu.VMEM((7, HALF + 2, Y_DEV + 2, *TILE), F32),
-            pltpu.VMEM((7, 2, Y_DEV + 2, *TILE), F32),
+            pltpu.VMEM((steps, *RIM), F32),
+            pltpu.VMEM((steps, 2, Y_DEV + 2, *TILE), F32),
             pltpu.VMEM((2, HALF, Y_DEV, *TILE), F32),
             pltpu.VMEM((2, 2, HALF, *TILE), F32),
             pltpu.VMEM((2, Y_DEV, *TILE), F32),
-            pltpu.SemaphoreType.DMA((7, 8)),
-            pltpu.SemaphoreType.DMA((7, 8)),
+            pltpu.SemaphoreType.DMA((steps, 8)),
+            pltpu.SemaphoreType.DMA((steps, 8)),
             pltpu.SemaphoreType.DMA((4,)),
             pltpu.SemaphoreType.DMA((4,)),
         ],
         5,
         32,
-        collective_id=0,
+        collective_id=1,
         has_side_effects=True,
-    )(rhs, inv, start.reshape(full.shape), yface, zface)
+    )(rhs, inv, start, yface, zface)
     return call(interleave_kernel, jax.ShapeDtypeStruct((Z_DEV, Y_DEV, NX), F32), [], 1, 16)(relaxed.reshape(-1, 128))
 
 

time: 73.8 us -> 70 us (0.949)
  blocking collectives: 22.7 us -> 0 us
  Pallas kernels: 47.8 us -> 63.6 us
  local copies, waits for them, and re-layouts: 2.94 us -> 6.02 us
    all_to_all x1 -> x0, blocking collectives: 22.7 us -> none  [shards(): lax.all_to_all(sent, ('slab', 'row'), split_axis=0, concat_axis=0, tiled=...]
    pallas_call x2, Pallas kernels: 35.3 us -> 51.1 us  [the longest x1 30.9 us: shards(): call(relax_kernel, full, [pltpu.VMEM((steps, *RIM), F32), pltpu.VMEM((ste...]
    unnamed x18 -> x14, local copies, waits for them, and re-layouts: 2.94 us -> 6.02 us
where the time goes in v1:
time: 70 us; the launch traced here: 69.6 us
  Pallas kernels  63.6 us (91%)
  local copies, waits for them, and re-layouts  6.02 us (9%)
    pallas_call x1, Pallas kernels, shards(): call(relax_kernel, full, [pltpu.VMEM((steps, *RIM), F32), pltpu.VMEM((ste...  30.9 us
    pallas_call x1, Pallas kernels, shards(): call(bin_kernel, (jax.ShapeDtypeStruct((peers * 8, 128), F32), jax.ShapeD...  20.2 us
    pallas_call x1, Pallas kernels, shards(): call(splat_kernel, outs, [pltpu.VMEM((Z_DEV * Y_DEV, 32, 128), F32), pltp...  11 us
    unnamed x14, local copies, waits for them, and re-layouts  6.02 us
    pallas_call x1, Pallas kernels, shards(): call(interleave_kernel, jax.ShapeDtypeStruct((Z_DEV, Y_DEV, NX), F32), []...  1.49 us

profile of v1, /device:TPU:7, one launch (start us, length us, event | category | flops | bytes accessed | tf_op | source)
XLA Modules:
  0.0 69.6 jit_solution(2270357647832677164)
XLA Ops:
  0.0 0.0 copy-start
  0.0 1.2 %copy-done = f32[16,16,1024]{2,1,0:T(8,128)S(1)} copy-done((f32[16,16,1024]{2,1,0:T(8,128)S(1)}, f32[16,16,1024]{2,1,0:T(8,128)}, u32[]{:S(2)}) %copy-start) | copy-done | bytes 1048600
  1.2 0.0 copy-start.1
  1.2 0.9 %copy-done.1 = f32[1,128,2,3,64]{1,4,3,2,0:T(8,128)S(1)} copy-done((f32[1,128,2,3,64]{1,4,3,2,0:T(8,128)S(1)}, f32[1,128,2,3,64]{1,4,3,2,0:T(8,128)}, u32[]{:S(2)}) %copy-start.1) | copy-done | bytes 196632
  2.2 0.0 copy-start.2
  2.2 0.8 %copy-done.2 = s32[1,128,2,64]{1,3,2,0:T(8,128)S(1)} copy-done((s32[1,128,2,64]{1,3,2,0:T(8,128)S(1)}, s32[1,128,2,64]{1,3,2,0:T(8,128)}, u32[]{:S(2)}) %copy-start.2) | copy-done | bytes 65560
  3.0 0.0 copy-start.3
  3.0 0.8 %copy-done.3 = f32[1,128,2,64]{1,3,2,0:T(8,128)S(1)} copy-done((f32[1,128,2,64]{1,3,2,0:T(8,128)S(1)}, f32[1,128,2,64]{1,3,2,0:T(8,128)}, u32[]{:S(2)}) %copy-start.3) | copy-done | bytes 65560
  3.8 0.0 copy-start.4
  3.8 0.8 %copy-done.4 = f32[1,128,2,64]{1,3,2,0:T(8,128)S(1)} copy-done((f32[1,128,2,64]{1,3,2,0:T(8,128)S(1)}, f32[1,128,2,64]{1,3,2,0:T(8,128)}, u32[]{:S(2)}) %copy-start.4) | copy-done | bytes 65560
  4.7 0.0 copy-start.5
  4.7 0.7 copy-done.5
  5.4 0.0 copy-start.6
  5.4 0.7 copy-done.6
  6.0 20.2 %shard_map.73 = (f32[1024,128]{1,0:T(8,128)S(1)}, f32[2,10,18,8,128]{4,3,2,1,0:T(8,128)S(1)}) custom-call(s32[2,128]{1,0:T(2,128)S(1)} %bitcast.24, s32[2,128]{1,0:T(2,128)S(1)} %bitcast.25, s32[2,64,128]{2,1,0:T(8,128)S(1)} %bitcast.21, f32[2,64,128]{2,1,0:T(8,128)S(1)} %bitcast.22, f32[2,3,64,128]{3,2,1,0:T(8,128)S(1)} %bitcast.20, ...), custom_call_target="tpu_custom_call" | custom-call | tf_op jit(solution)/shard_map/pallas_call | solution.py:474
  26.2 11.0 %shard_map.74 = (f32[2,8,16,8,128]{4,3,2,1,0:T(8,128)S(1)}, f32[2,8,16,8,128]{4,3,2,1,0:T(8,128)S(1)}, f32[2,2,8,8,128]{4,3,2,1,0:T(8,128)S(1)}, f32[2,16,8,128]{3,2,1,0:T(8,128)S(1)}) custom-call(f32[1024,128]{1,0:T(8,128)S(1)} %get-tuple-element.11.points_ref), custom_call_target="tpu_custom_call" | custom-call | tf_op jit(solution)/shard_map/pallas_call | solution.py:497
  37.2 30.9 %shard_map.75 = f32[2,8,16,8,128]{4,3,2,1,0:T(8,128)S(1)} custom-call(f32[2,8,16,8,128]{4,3,2,1,0:T(8,128)S(1)} %get-tuple-element.12.rhs_in, f32[2,8,16,8,128]{4,3,2,1,0:T(8,128)S(1)} %get-tuple-element.13.inv_ref, f32[2,10,18,8,128]{4,3,2,1,0:T(8,128)S(1)} %get-tuple-element.14.start_ref, f32[2,2,8,8,128]{4,3,2,1,0:T(8,128)S(1)} %get-tuple-element.15.yface_ref, ...), custom_call_target="tpu_custom_call" | custom-call | tf_op jit(solution)/shard_map/pallas_call | solution.py:511
  68.1 1.5 %shard_map.76 = f32[16,16,1024]{2,1,0:T(8,128)} custom-call(f32[2048,128]{1,0:T(8,128)S(1)} %bitcast.19), custom_call_target="tpu_custom_call" | custom-call | tf_op jit(solution)/shard_map/pallas_call | solution.py:530
Async XLA Ops:
  0.0 1.2 %copy-start = (f32[16,16,1024]{2,1,0:T(8,128)S(1)}, f32[16,16,1024]{2,1,0:T(8,128)}, u32[]{:S(2)}) copy-start(f32[16,16,1024]{2,1,0:T(8,128)} %guess_ref.1) | copy-start | bytes 3145732
  1.2 0.9 %copy-start.1 = (f32[1,128,2,3,64]{1,4,3,2,0:T(8,128)S(1)}, f32[1,128,2,3,64]{1,4,3,2,0:T(8,128)}, u32[]{:S(2)}) copy-start(f32[1,128,2,3,64]{1,4,3,2,0:T(8,128)} %param.11) | copy-start | bytes 589828
  2.2 0.8 %copy-start.2 = (s32[1,128,2,64]{1,3,2,0:T(8,128)S(1)}, s32[1,128,2,64]{1,3,2,0:T(8,128)}, u32[]{:S(2)}) copy-start(s32[1,128,2,64]{1,3,2,0:T(8,128)} %param.9) | copy-start | bytes 196612
  3.0 0.8 %copy-start.3 = (f32[1,128,2,64]{1,3,2,0:T(8,128)S(1)}, f32[1,128,2,64]{1,3,2,0:T(8,128)}, u32[]{:S(2)}) copy-start(f32[1,128,2,64]{1,3,2,0:T(8,128)} %param.10) | copy-start | bytes 196612
  3.8 0.8 %copy-start.4 = (f32[1,128,2,64]{1,3,2,0:T(8,128)S(1)}, f32[1,128,2,64]{1,3,2,0:T(8,128)}, u32[]{:S(2)}) copy-start(f32[1,128,2,64]{1,3,2,0:T(8,128)} %param.12) | copy-start | bytes 196612
  4.7 0.7 copy-start.5
  5.4 0.7 copy-start.6

commit v2 on v1

--- a/solution.py
+++ b/solution.py
@@ -16,6 +16,7 @@
 HALF = Z_DEV // 2
 TILE = (8, 128)
 MESH = pl.DeviceIdType.MESH
+LOGICAL = pl.DeviceIdType.LOGICAL
 F32 = jnp.float32
 BF16 = jnp.bfloat16
 I32 = jnp.int32
@@ -76,7 +77,9 @@
                 start_ref[pl.ds(base, Y_DEV, stride=8), :] = colours[colour][z * Y_DEV : (z + 1) * Y_DEV]
 
 
-SIDES = [(0, 1), (0, -1), (1, 0), (-1, 0), (1, 1), (1, -1), (-1, 1), (-1, -1)]
+SIDES = [(1, 1), (1, -1), (-1, 1), (-1, -1), (1, 0), (-1, 0), (0, 1), (0, -1)]
+FACES = SIDES[4:]
+EDGE = (2, HALF + 2, *TILE)
 LAST = Y_DEV + 1
 RIM = (HALF + 2, Y_DEV + 2, *TILE)
 
@@ -138,32 +141,64 @@
                     y = 0 if d[1] == 1 else LAST
                     tiles[1 : HALF + 1, y : y + 1] = jnp.zeros((HALF, 1, *TILE), F32)
                 else:
-                    at, size = {0: (1, Y_DEV), 1: (0, 1), -1: (LAST, 1)}[d[1]]
+                    at, size = EDGE_AT[d[1]]
                     edge[0 if d[0] == 1 else 1, at : at + size] = jnp.zeros((size, *TILE), F32)
 
-    def halo(self, tiles, edge, send, recv):
-        spans = {0: (pl.ds(1, Y_DEV), pl.ds(1, Y_DEV)), 1: (pl.ds(Y_DEV, 1), pl.ds(0, 1)), -1: (pl.ds(1, 1), pl.ds(LAST, 1))}
+    def halo(self, tiles, edge, face, send, recv):
         pairs = []
         for q, d in enumerate(SIDES):
-            src_y, dst_y = spans[d[1]]
+            at, size = EDGE_AT[d[1]]
+            side = 0 if d[0] == 1 else 1
             if d[0] == 0:
-                src, dst = tiles.at[pl.ds(1, HALF), src_y], tiles.at[pl.ds(1, HALF), dst_y]
+                src, dst = (tiles.at[pl.ds(1, HALF), pl.ds(y, 1)] for y in ((Y_DEV, 0) if d[1] == 1 else (1, LAST)))
+            elif d[1] == 0:
+                src, dst = face.at[side], edge.at[side, pl.ds(at, size)]
             else:
-                src, dst = tiles.at[HALF if d[0] == 1 else 1, src_y], edge.at[0 if d[0] == 1 else 1, dst_y]
+                src = tiles.at[HALF if d[0] == 1 else 1, pl.ds(Y_DEV if d[1] == 1 else 1, 1)]
+                dst = edge.at[side, pl.ds(at, size)]
             pairs.append((d, pltpu.make_async_remote_copy(src, dst, send.at[q], recv.at[q], self.device(d), MESH)))
         return pairs
 
 
+EDGE_AT = {0: (0, HALF), 1: (HALF, 1), -1: (HALF + 1, 1)}
+
+
+def pack_faces(tiles, face):
+    low = low_half((HALF, *TILE))
+    face[0] = jnp.where(low, swap_halves(tiles[HALF, 1 : HALF + 1]), tiles[HALF, HALF + 1 : LAST])
+    face[1] = jnp.where(low, tiles[1, 1 : HALF + 1], swap_halves(tiles[1, HALF + 1 : LAST]))
+
+
 def rims(tiles, edge):
-    low = low_half((Y_DEV + 2, *TILE))
-    tiles[0] = swap_halves(jnp.where(low, tiles[HALF], edge[0]))
-    tiles[HALF + 1] = swap_halves(jnp.where(low, edge[1], tiles[1]))
+    low = low_half((HALF, *TILE))
+    top, bottom = tiles[HALF], tiles[1]
+    below, above = edge[0], edge[1]
+    first, second = slice(1, HALF + 1), slice(HALF + 1, LAST)
+    tiles[0, first] = jnp.where(low, below[:HALF], swap_halves(top[first]))
+    tiles[0, second] = swap_halves(jnp.where(low, top[second], below[:HALF]))
+    tiles[HALF + 1, first] = swap_halves(jnp.where(low, above[:HALF], bottom[first]))
+    tiles[HALF + 1, second] = jnp.where(low, swap_halves(bottom[second]), above[:HALF])
+    for y, at in ((slice(0, 1), HALF), (slice(LAST, LAST + 1), HALF + 1)):
+        tiles[0, y] = swap_halves(jnp.where(low[:1], top[y], below[at : at + 1]))
+        tiles[HALF + 1, y] = swap_halves(jnp.where(low[:1], above[at : at + 1], bottom[y]))
 
 
 def bin_kernel(
-    brick_ref, count_ref, cell_ref, frac_ref, normal_ref, weight_ref, guess_ref, points_ref, v_ref,
-    packed, split, edge, psend, precv, send, recv,
+    brick_in, count_in, cell_in, frac_in, normal_in, weight_in, guess_in, points_ref, v_ref,
+    brick_ref, count_ref, cell_ref, frac_ref, normal_ref, weight_ref, guess_ref,
+    packed, split, edge, face, load, psend, precv, send, recv,
 ):
+    loads = [
+        pltpu.make_async_copy(src, dst, load.at[q])
+        for q, (src, dst) in enumerate(
+            (
+                (guess_in, guess_ref), (brick_in, brick_ref), (count_in, count_ref), (cell_in, cell_ref),
+                (frac_in, frac_ref), (normal_in, normal_ref), (weight_in, weight_ref),
+            )
+        )
+    ]
+    for copy in loads:
+        copy.start()
     grid = Grid()
     peers = grid.ns * grid.nr
     me = grid.slab * grid.nr + grid.line
@@ -172,14 +207,23 @@
         grid.clear_outside(v_ref.at[colour], edge.at[colour])
 
     def peer(i):
-        t = lax.rem(me + i, peers)
-        return t, (t // grid.nr, lax.rem(t, grid.nr))
+        return lax.rem(me + lax.rem(i + peers // 2 - 1, peers - 1) + 1, peers)
 
     def greet(i, _):
-        pl.semaphore_signal(barrier, inc=1, device_id=peer(i)[1], device_id_type=MESH)
+        pl.semaphore_signal(barrier, inc=1, device_id=peer(i), device_id_type=LOGICAL)
         return 0
 
-    lax.fori_loop(1, peers, greet, 0)
+    lax.fori_loop(0, peers - 1, greet, 0)
+
+    loads[0].wait()
+    deinterleave(guess_ref, split)
+    for colour in range(2):
+        for zp in range(HALF):
+            at = (colour * HALF + zp) * Y_DEV * 8
+            v_ref[colour, zp + 1, 1:LAST] = split[at : at + Y_DEV * 8, :].reshape(Y_DEV, *TILE)
+        pack_faces(v_ref.at[colour], face.at[colour])
+    for copy in loads[1:]:
+        copy.wait()
 
     point = iota((CAP, peers), 0)
     live = jnp.concatenate([(point < count_ref[s : s + 1, :]).astype(F32) for s in range(S_PEER)], axis=0)
@@ -202,25 +246,20 @@
     pl.semaphore_wait(barrier, peers - 1)
 
     def send_points(i, _):
-        t, device = peer(i)
-        pltpu.make_async_remote_copy(packed.at[tile(t)], points_ref.at[tile(me)], psend, precv, device, MESH).start()
+        t = peer(i)
+        pltpu.make_async_remote_copy(packed.at[tile(t)], points_ref.at[tile(me)], psend, precv, t, LOGICAL).start()
         return 0
 
-    lax.fori_loop(1, peers, send_points, 0)
+    lax.fori_loop(0, peers - 1, send_points, 0)
+    halos = [grid.halo(v_ref.at[c], edge.at[c], face.at[c], send.at[c], recv.at[c]) for c in range(2)]
+    for colour in range(2):
+        grid.start(halos[colour])
     points_ref[tile(me), :] = packed[tile(me), :]
-    deinterleave(guess_ref, split)
-    for colour in range(2):
-        for zp in range(HALF):
-            at = (colour * HALF + zp) * Y_DEV * 8
-            v_ref[colour, zp + 1, 1:LAST] = split[at : at + Y_DEV * 8, :].reshape(Y_DEV, *TILE)
-    halos = [grid.halo(v_ref.at[c], edge.at[c], send.at[c], recv.at[c]) for c in range(2)]
-    for colour in range(2):
-        grid.start(halos[colour])
     for colour in range(2):
         grid.take(halos[colour])
         rims(v_ref.at[colour], edge.at[colour])
     others = pl.ds(0, (peers - 1) * 8)
-    every = pltpu.make_async_remote_copy(packed.at[others], points_ref.at[others], psend, precv, peer(1)[1], MESH)
+    every = pltpu.make_async_remote_copy(packed.at[others], points_ref.at[others], psend, precv, peer(0), LOGICAL)
     every.wait_recv()
     every.wait_send()
     for colour in range(2):
@@ -276,18 +315,24 @@
         wa, wb = both(wm, beyond), both(beside, zero)
         vals = [both(v, v) for v in (n0, n1, n2, w)]
         for r in range(8):
+            weights, onehots = [], []
             for s in range(S_PEER):
                 def row(x):
                     return x[s][r : r + 1, :]
 
                 unit = jnp.where(rank == row(ha), row(wa), jnp.where(rank == row(hb), row(wb), 0.0))
-                a = jnp.concatenate([unit * row(v) for v in vals], axis=0)
-                onehot = (wide_rank == row(lanes_)).astype(F32).astype(BF16)
-                out = lax.dot_general(
-                    jnp.concatenate(parts(a), axis=0), onehot, (((1,), (1,)), ((), ())), preferred_element_type=F32
-                )
+                weights.append(jnp.concatenate(parts(jnp.concatenate([unit * row(v) for v in vals], axis=0)), axis=0))
+                onehots.append((wide_rank == row(lanes_)).astype(F32).astype(BF16))
+            apart = jnp.zeros(weights[0].shape, BF16)
+            diagonal = jnp.concatenate(
+                [jnp.concatenate([weights[0], apart], axis=1), jnp.concatenate([apart, weights[1]], axis=1)], axis=0
+            )
+            out = lax.dot_general(
+                diagonal, jnp.concatenate(onehots, axis=1), (((1,), (1,)), ((), ())), preferred_element_type=F32
+            )
+            for s in range(S_PEER):
                 b = brick_s[g * 8 + r, s * CAP]
-                acc[b] = acc[b] + (out[:32] + out[32:])
+                acc[b] = acc[b] + (out[s * 64 : s * 64 + 32] + out[s * 64 + 32 : s * 64 + 64])
         return 0
 
     lax.fori_loop(0, sources // 8, group, 0)
@@ -342,7 +387,7 @@
     lax.fori_loop(0, HALF, finish, 0)
 
 
-def relax_kernel(rhs_in, inv_ref, start_ref, yface_ref, zface_ref, out_ref, v, edge, rhs, yin, zfin, send, recv, fsend, frecv):
+def relax_kernel(rhs_in, inv_ref, start_ref, yface_ref, zface_ref, out_ref, v, edge, rhs, yin, zfin, face, send, recv, fsend, frecv):
     grid = Grid()
     versions = [start_ref.at[0], start_ref.at[1]] + [v.at[n] for n in range(2 * SWEEPS - 1)]
 
@@ -350,30 +395,70 @@
         grid.clear_outside(v.at[n], edge.at[n])
         return 0
 
+    grid.greet_neighbours()
     lax.fori_loop(0, 2 * SWEEPS - 1, clear, 0)
-    for q, d in enumerate(SIDES[:4]):
-        s = 0 if d[q < 2] == 1 else 1
+    for d in FACES:
+        s = 0 if sum(d) == 1 else 1
+
         @pl.when(jnp.logical_not(grid.exists((-d[0], -d[1]))))
         def _():
             if d[0] == 0:
                 yin[s] = jnp.zeros(yin.shape[1:], F32)
             else:
                 zfin[s] = jnp.zeros(zfin.shape[1:], F32)
-    grid.greet_neighbours()
+
+    def update(step, zp, y, count):
+        zp, parity = (zp, zp) if isinstance(zp, int) else zp
+        same, opp, colour = versions[step], versions[step + 1], step % 2
+        outer = count == 1 or (isinstance(zp, int) and zp in (0, HALF - 1))
+        right = (rhs if outer else rhs_in)[colour, zp, y : y + count]
+        parity = (parity + y + colour) % 2
+        s1 = same[zp, y : y + count + 2] + same[zp + 2, y : y + count + 2]
+        o1 = opp[zp, y : y + count + 2] + opp[zp + 2, y : y + count + 2]
+        s0 = same[zp + 1, y : y + count + 2]
+        around = s1[1:-1] + s0[:-2] + s0[2:]
+        diagonal = s1[:-2] + s1[2:]
+        across = 2.0 * around + (o1[:-2] + o1[2:])
+        total = right + 2.0 * diagonal + across
+        other = neighbour(across, parity) if count == 1 else by_rows(across, parity, neighbour)
+        value = (total + other) * inv_ref[colour, zp, y : y + count]
+        if step < 2 * SWEEPS - 1:
+            versions[step + 2][zp + 1, y + 1 : y + 1 + count] = value
+        if step >= 2 * SWEEPS - 2:
+            out_ref[colour, zp, y : y + count] = value
+
+    def inner(step):
+        def planes(pair, _):
+            for odd in range(2):
+                update(step, (pair * 2 + 1 + odd, 1 + odd), 1, Y_DEV - 2)
+            return 0
+
+        lax.fori_loop(0, HALF // 2 - 1, planes, 0)
+
+    def outer(step):
+        for zp in (0, HALF - 1):
+            update(step, zp, 0, Y_DEV)
+        for zp in range(1, HALF - 1):
+            for y in (0, Y_DEV - 1):
+                update(step, zp, y, 1)
+
+    faces = []
+    for q, d in enumerate(FACES):
+        s = 0 if sum(d) == 1 else 1
+        src, dst = (yface_ref, yin) if d[0] == 0 else (zface_ref, zfin)
+        faces.append(
+            (d, pltpu.make_async_remote_copy(src.at[1 - s], dst.at[s], fsend.at[q], frecv.at[q], grid.device(d), MESH))
+        )
+    inner(0)
     grid.await_neighbours()
-    faces = []
-    for q, d in enumerate(SIDES[:4]):
-        s = 0 if d[q < 2] == 1 else 1
-        if d[0] == 0:
-            src, dst = yface_ref.at[1 - s], yin.at[s]
-        else:
-            src, dst = zface_ref.at[1 - s], zfin.at[s]
-        faces.append((d, pltpu.make_async_remote_copy(src, dst, fsend.at[q], frecv.at[q], grid.device(d), MESH)))
     grid.start(faces)
-    for colour in range(2):
-        for zp in range(HALF):
+    low = low_half((Y_DEV, *TILE))
+    for colour in range(2):
+        for zp in (0, HALF - 1):
             rhs[colour, zp] = rhs_in[colour, zp]
-    low = low_half((Y_DEV, *TILE))
+        for zp in range(1, HALF - 1):
+            for y in (0, Y_DEV - 1):
+                rhs[colour, zp, y] = rhs_in[colour, zp, y]
     grid.take(faces)
     for colour in range(2):
         for zp in range(HALF):
@@ -387,43 +472,16 @@
 
     sent = [faces]
     for step in range(2 * SWEEPS):
-        same, opp, colour = versions[step], versions[step + 1], step % 2
-        new = versions[step + 2] if step < 2 * SWEEPS - 1 else None
-
-        def update(zp, y, count):
-            parity = (zp if isinstance(zp, int) else zp[1]) + y + colour
-            zp = zp if isinstance(zp, int) else zp[0]
-            s1 = same[zp, y : y + count + 2] + same[zp + 2, y : y + count + 2]
-            o1 = opp[zp, y : y + count + 2] + opp[zp + 2, y : y + count + 2]
-            s0 = same[zp + 1, y : y + count + 2]
-            around = s1[1:-1] + s0[:-2] + s0[2:]
-            diagonal = s1[:-2] + s1[2:]
-            across = 2.0 * around + (o1[:-2] + o1[2:])
-            total = rhs[colour, zp, y : y + count] + 2.0 * diagonal + across
-            other = neighbour(across, parity % 2) if count == 1 else by_rows(across, parity % 2, neighbour)
-            value = (total + other) * inv_ref[colour, zp, y : y + count]
-            if new is not None:
-                new[zp + 1, y + 1 : y + 1 + count] = value
-            if step >= 2 * SWEEPS - 2:
-                out_ref[colour, zp, y : y + count] = value
-
-        for zp in range(1, HALF - 1):
-            for y in (0, Y_DEV - 1):
-                update(zp, y, 1)
-        for zp in (0, HALF - 1):
-            update(zp, 0, Y_DEV)
-        if new is not None:
-            pairs = grid.halo(new, edge.at[step], send.at[step], recv.at[step])
+        outer(step)
+        if step < 2 * SWEEPS - 1:
+            new = versions[step + 2]
+            pack_faces(new, face.at[step])
+            pairs = grid.halo(new, edge.at[step], face.at[step], send.at[step], recv.at[step])
             grid.start(pairs)
             sent.append(pairs)
-
-        def inner(pair, _):
-            for odd in range(2):
-                update((pair * 2 + 1 + odd, 1 + odd), 1, Y_DEV - 2)
-            return 0
-
-        lax.fori_loop(0, HALF // 2 - 1, inner, 0)
-        if new is not None:
+        if step > 0:
+            inner(step)
+        if step < 2 * SWEEPS - 1:
             grid.take(pairs)
             rims(new, edge.at[step])
 
@@ -452,11 +510,11 @@
 VM = pl.BlockSpec(memory_space=pltpu.VMEM)
 
 
-def call(kernel, outs, scratch, count, limit, **params):
+def call(kernel, outs, scratch, specs, limit, **params):
     return pl.pallas_call(
         kernel,
         out_shape=outs,
-        in_specs=[VM] * count,
+        in_specs=specs,
         out_specs=jax.tree.map(lambda _: VM, outs),
         scratch_shapes=scratch,
         compiler_params=pltpu.CompilerParams(vmem_limit_bytes=limit << 20, **params),
@@ -471,23 +529,27 @@
     def last(x):
         return jnp.moveaxis(x[0], 0, -1)
 
+    args = (last(slot_brick), last(slot_count), last(point_cell), last(point_frac), last(point_normal), last(point_weight), guess)
     points, start = call(
         bin_kernel,
         (jax.ShapeDtypeStruct((peers * 8, 128), F32), jax.ShapeDtypeStruct((2, *RIM), F32)),
-        [
+        [pltpu.VMEM(a.shape, a.dtype) for a in args]
+        + [
             pltpu.VMEM((peers * 8, 128), F32),
             pltpu.VMEM((2 * HALF * Y_DEV * 8, 128), F32),
-            pltpu.VMEM((2, 2, Y_DEV + 2, *TILE), F32),
+            pltpu.VMEM((2, *EDGE), F32),
+            pltpu.VMEM((2, 2, HALF, *TILE), F32),
+            pltpu.SemaphoreType.DMA((7,)),
             pltpu.SemaphoreType.DMA,
             pltpu.SemaphoreType.DMA,
             pltpu.SemaphoreType.DMA((2, 8)),
             pltpu.SemaphoreType.DMA((2, 8)),
         ],
-        7,
+        [pl.BlockSpec(memory_space=pltpu.HBM)] * 7,
         24,
         collective_id=0,
         has_side_effects=True,
-    )(last(slot_brick), last(slot_count), last(point_cell), last(point_frac), last(point_normal), last(point_weight), guess)
+    )(*[pltpu.with_memory_space_constraint(a, pltpu.HBM) for a in args])
     outs = (
         full,
         full,
@@ -505,7 +567,7 @@
             pltpu.VMEM((2, HALF + 2, Y_DEV, *TILE), F32),
             pltpu.SemaphoreType.DMA,
         ],
-        1,
+        [VM],
         32,
     )(points)
     relaxed = call(
@@ -513,21 +575,22 @@
         full,
         [
             pltpu.VMEM((steps, *RIM), F32),
-            pltpu.VMEM((steps, 2, Y_DEV + 2, *TILE), F32),
+            pltpu.VMEM((steps, *EDGE), F32),
             pltpu.VMEM((2, HALF, Y_DEV, *TILE), F32),
             pltpu.VMEM((2, 2, HALF, *TILE), F32),
             pltpu.VMEM((2, Y_DEV, *TILE), F32),
+            pltpu.VMEM((steps, 2, HALF, *TILE), F32),
             pltpu.SemaphoreType.DMA((steps, 8)),
             pltpu.SemaphoreType.DMA((steps, 8)),
             pltpu.SemaphoreType.DMA((4,)),
             pltpu.SemaphoreType.DMA((4,)),
         ],
-        5,
+        [VM] * 5,
         32,
         collective_id=1,
         has_side_effects=True,
     )(rhs, inv, start, yface, zface)
-    return call(interleave_kernel, jax.ShapeDtypeStruct((Z_DEV, Y_DEV, NX), F32), [], 1, 16)(relaxed.reshape(-1, 128))
+    return call(interleave_kernel, jax.ShapeDtypeStruct((Z_DEV, Y_DEV, NX), F32), [], [VM], 16)(relaxed.reshape(-1, 128))
 
 
 def solution(mesh):

time: 70 us -> 59.8 us (0.85)
  local copies, waits for them, and re-layouts: 6.02 us -> 0 us
  Pallas kernels: 63.6 us -> 59.6 us
    unnamed x14 -> x0, local copies, waits for them, and re-layouts: 6.02 us -> none
    pallas_call x1, Pallas kernels: 11 us -> 8.97 us  [shards(): call(splat_kernel, outs, [pltpu.VMEM((Z_DEV * Y_DEV, 32, 128), F32), pltp...]
    pallas_call x1, Pallas kernels: 30.9 us -> 28.9 us  [shards(): call(relax_kernel, full, [pltpu.VMEM((steps, *RIM), F32), pltpu.VMEM((ste...]
where the time goes in v2:
time: 59.8 us; the launch traced here: 59.7 us
  Pallas kernels  59.6 us (100%)
    pallas_call x1, Pallas kernels, shards(): call(relax_kernel, full, [pltpu.VMEM((steps, *RIM), F32), pltpu.VMEM((ste...  28.9 us
    pallas_call x1, Pallas kernels, shards(): call(bin_kernel, (jax.ShapeDtypeStruct((peers * 8, 128), F32), jax.ShapeD...  20.3 us
    pallas_call x1, Pallas kernels, shards(): call(splat_kernel, outs, [pltpu.VMEM((Z_DEV * Y_DEV, 32, 128), F32), pltp...  8.97 us
    pallas_call x1, Pallas kernels, shards(): call(interleave_kernel, jax.ShapeDtypeStruct((Z_DEV, Y_DEV, NX), F32), []...  1.49 us

profile of v2, /device:TPU:7, one launch (start us, length us, event | category | flops | bytes accessed | tf_op | source)
XLA Modules:
  0.0 59.7 jit_solution(16553122402121281110)
XLA Ops:
  0.0 20.3 %shard_map.73 = (f32[1024,128]{1,0:T(8,128)S(1)}, f32[2,10,18,8,128]{4,3,2,1,0:T(8,128)S(1)}) custom-call(s32[2,128]{1,0:T(2,128)} %bitcast.24, s32[2,128]{1,0:T(2,128)} %bitcast.25, s32[2,64,128]{2,1,0:T(8,128)} %bitcast.21, f32[2,64,128]{2,1,0:T(8,128)} %bitcast.22, f32[2,3,64,128]{3,2,1,0:T(8,128)} %bitcast.20, f32[2,64,128]{2,1,0:T(8,128)} %bitcast.23, ...), custom_call_target="tpu_custom_call" | custom-call | tf_op jit(solution)/shard_map/pallas_call | solution.py:533
  20.3 9.0 %shard_map.74 = (f32[2,8,16,8,128]{4,3,2,1,0:T(8,128)S(1)}, f32[2,8,16,8,128]{4,3,2,1,0:T(8,128)S(1)}, f32[2,2,8,8,128]{4,3,2,1,0:T(8,128)S(1)}, f32[2,16,8,128]{3,2,1,0:T(8,128)S(1)}) custom-call(f32[1024,128]{1,0:T(8,128)S(1)} %get-tuple-element.11.points_ref), custom_call_target="tpu_custom_call" | custom-call | tf_op jit(solution)/shard_map/pallas_call | solution.py:559
  29.3 28.9 %shard_map.75 = f32[2,8,16,8,128]{4,3,2,1,0:T(8,128)S(1)} custom-call(f32[2,8,16,8,128]{4,3,2,1,0:T(8,128)S(1)} %get-tuple-element.12.rhs_in, f32[2,8,16,8,128]{4,3,2,1,0:T(8,128)S(1)} %get-tuple-element.13.inv_ref, f32[2,10,18,8,128]{4,3,2,1,0:T(8,128)S(1)} %get-tuple-element.14.start_ref, f32[2,2,8,8,128]{4,3,2,1,0:T(8,128)S(1)} %get-tuple-element.15.yface_ref, ...), custom_call_target="tpu_custom_call" | custom-call | tf_op jit(solution)/shard_map/pallas_call | solution.py:573
  58.2 1.5 %shard_map.76 = f32[16,16,1024]{2,1,0:T(8,128)} custom-call(f32[2048,128]{1,0:T(8,128)S(1)} %bitcast.19), custom_call_target="tpu_custom_call" | custom-call | tf_op jit(solution)/shard_map/pallas_call | solution.py:593

commit v3 on v2

--- a/solution.py
+++ b/solution.py
@@ -78,10 +78,16 @@
 
 
 SIDES = [(1, 1), (1, -1), (-1, 1), (-1, -1), (1, 0), (-1, 0), (0, 1), (0, -1)]
-FACES = SIDES[4:]
-EDGE = (2, HALF + 2, *TILE)
-LAST = Y_DEV + 1
-RIM = (HALF + 2, Y_DEV + 2, *TILE)
+WIDE = 2
+FULL = (HALF, Y_DEV, *TILE)
+
+
+def rimmed(width):
+    return (HALF + 2 * width, Y_DEV + 2 * width, *TILE)
+
+
+def edge_shape(width):
+    return (2, width, HALF + 2 * width, *TILE)
 
 
 class Grid:
@@ -133,54 +139,82 @@
             def _():
                 copy.wait_send()
 
-    def clear_outside(self, tiles, edge):
-        for d in SIDES:
+    def clear(self, pairs):
+        for d, dst in pairs:
             @pl.when(jnp.logical_not(self.exists((-d[0], -d[1]))))
             def _():
-                if d[0] == 0:
-                    y = 0 if d[1] == 1 else LAST
-                    tiles[1 : HALF + 1, y : y + 1] = jnp.zeros((HALF, 1, *TILE), F32)
-                else:
-                    at, size = EDGE_AT[d[1]]
-                    edge[0 if d[0] == 1 else 1, at : at + size] = jnp.zeros((size, *TILE), F32)
-
-    def halo(self, tiles, edge, face, send, recv):
-        pairs = []
-        for q, d in enumerate(SIDES):
-            at, size = EDGE_AT[d[1]]
+                dst[...] = jnp.zeros(dst.shape, F32)
+
+    def halo(self, tiles, edge, face, beside=None):
+        w = WIDE
+        ends = {1: pl.ds(Y_DEV, w), -1: pl.ds(w, w)}
+        plan = []
+        for d in SIDES:
             side = 0 if d[0] == 1 else 1
             if d[0] == 0:
-                src, dst = (tiles.at[pl.ds(1, HALF), pl.ds(y, 1)] for y in ((Y_DEV, 0) if d[1] == 1 else (1, LAST)))
+                dst = tiles.at[pl.ds(w, HALF), pl.ds(0 if d[1] == 1 else Y_DEV + w, w)]
+                if beside is not None:
+                    dst = beside.at[0 if d[1] == 1 else 1]
+                plan.append((d, tiles.at[pl.ds(w, HALF), ends[d[1]]], dst))
             elif d[1] == 0:
-                src, dst = face.at[side], edge.at[side, pl.ds(at, size)]
+                plan.append((d, face.at[side], edge.at[side, pl.ds(0, w), pl.ds(0, HALF)]))
             else:
-                src = tiles.at[HALF if d[0] == 1 else 1, pl.ds(Y_DEV if d[1] == 1 else 1, 1)]
-                dst = edge.at[side, pl.ds(at, size)]
-            pairs.append((d, pltpu.make_async_remote_copy(src, dst, send.at[q], recv.at[q], self.device(d), MESH)))
-        return pairs
-
-
-EDGE_AT = {0: (0, HALF), 1: (HALF, 1), -1: (HALF + 1, 1)}
+                dst = edge.at[side, pl.ds(0, w), pl.ds(HALF if d[1] == 1 else HALF + w, w)]
+                plan.append((d, tiles.at[pl.ds(HALF if d[0] == 1 else w, w), ends[d[1]]], dst))
+        return plan
+
+    def copies(self, plan, send, recv):
+        return [
+            (d, pltpu.make_async_remote_copy(src, dst, send.at[q], recv.at[q], self.device(d), MESH))
+            for q, (d, src, dst) in enumerate(plan)
+        ]
+
+
+def landing(plan):
+    return [(d, dst) for d, _, dst in plan]
+
+
+def pack_top(first, second):
+    return jnp.where(low_half(first.shape), swap_halves(first), second)
+
+
+def pack_bottom(first, second):
+    return jnp.where(low_half(first.shape), first, swap_halves(second))
 
 
 def pack_faces(tiles, face):
+    w, half = WIDE, WIDE + HALF
+    for p in range(w):
+        face[0, p] = pack_top(tiles[HALF + p, w:half], tiles[HALF + p, half : half + HALF])
+        face[1, p] = pack_bottom(tiles[w + p, w:half], tiles[w + p, half : half + HALF])
+
+
+def under(own, corner):
+    return swap_halves(jnp.where(low_half(own.shape), own, corner))
+
+
+def over(own, corner):
+    return swap_halves(jnp.where(low_half(own.shape), corner, own))
+
+
+def rim_planes(tiles, w, p, below, above):
+    half = w + HALF
+    first, second = slice(w, half), slice(half, half + HALF)
+    top, bottom = tiles[HALF + p], tiles[w + p]
     low = low_half((HALF, *TILE))
-    face[0] = jnp.where(low, swap_halves(tiles[HALF, 1 : HALF + 1]), tiles[HALF, HALF + 1 : LAST])
-    face[1] = jnp.where(low, tiles[1, 1 : HALF + 1], swap_halves(tiles[1, HALF + 1 : LAST]))
+    up, down = p, HALF + w + p
+    tiles[up, first] = jnp.where(low, below[:HALF], swap_halves(top[first]))
+    tiles[up, second] = swap_halves(jnp.where(low, top[second], below[:HALF]))
+    tiles[down, first] = swap_halves(jnp.where(low, above[:HALF], bottom[first]))
+    tiles[down, second] = jnp.where(low, swap_halves(bottom[second]), above[:HALF])
+    for y, at in ((slice(0, w), slice(HALF, half)), (slice(Y_DEV + w, Y_DEV + 2 * w), slice(half, half + w))):
+        tiles[up, y] = under(top[y], below[at])
+        tiles[down, y] = over(bottom[y], above[at])
 
 
 def rims(tiles, edge):
-    low = low_half((HALF, *TILE))
-    top, bottom = tiles[HALF], tiles[1]
-    below, above = edge[0], edge[1]
-    first, second = slice(1, HALF + 1), slice(HALF + 1, LAST)
-    tiles[0, first] = jnp.where(low, below[:HALF], swap_halves(top[first]))
-    tiles[0, second] = swap_halves(jnp.where(low, top[second], below[:HALF]))
-    tiles[HALF + 1, first] = swap_halves(jnp.where(low, above[:HALF], bottom[first]))
-    tiles[HALF + 1, second] = jnp.where(low, swap_halves(bottom[second]), above[:HALF])
-    for y, at in ((slice(0, 1), HALF), (slice(LAST, LAST + 1), HALF + 1)):
-        tiles[0, y] = swap_halves(jnp.where(low[:1], top[y], below[at : at + 1]))
-        tiles[HALF + 1, y] = swap_halves(jnp.where(low[:1], above[at : at + 1], bottom[y]))
+    for p in range(WIDE):
+        rim_planes(tiles, WIDE, p, edge[0, p], edge[1, p])
 
 
 def bin_kernel(
@@ -203,11 +237,12 @@
     peers = grid.ns * grid.nr
     me = grid.slab * grid.nr + grid.line
     barrier = pltpu.get_barrier_semaphore()
-    for colour in range(2):
-        grid.clear_outside(v_ref.at[colour], edge.at[colour])
+    plans = [grid.halo(v_ref.at[c], edge.at[c], face.at[c]) for c in range(2)]
+    for plan in plans:
+        grid.clear(landing(plan))
 
     def peer(i):
-        return lax.rem(me + lax.rem(i + peers // 2 - 1, peers - 1) + 1, peers)
+        return lax.rem(me + i + 1, peers)
 
     def greet(i, _):
         pl.semaphore_signal(barrier, inc=1, device_id=peer(i), device_id_type=LOGICAL)
@@ -220,7 +255,7 @@
     for colour in range(2):
         for zp in range(HALF):
             at = (colour * HALF + zp) * Y_DEV * 8
-            v_ref[colour, zp + 1, 1:LAST] = split[at : at + Y_DEV * 8, :].reshape(Y_DEV, *TILE)
+            v_ref[colour, zp + WIDE, WIDE : WIDE + Y_DEV] = split[at : at + Y_DEV * 8, :].reshape(Y_DEV, *TILE)
         pack_faces(v_ref.at[colour], face.at[colour])
     for copy in loads[1:]:
         copy.wait()
@@ -251,7 +286,7 @@
         return 0
 
     lax.fori_loop(0, peers - 1, send_points, 0)
-    halos = [grid.halo(v_ref.at[c], edge.at[c], face.at[c], send.at[c], recv.at[c]) for c in range(2)]
+    halos = [grid.copies(plans[c], send.at[c], recv.at[c]) for c in range(2)]
     for colour in range(2):
         grid.start(halos[colour])
     points_ref[tile(me), :] = packed[tile(me), :]
@@ -266,7 +301,7 @@
         grid.sent(halos[colour])
 
 
-def splat_kernel(points_ref, rhs_ref, inv_ref, yface_ref, zface_ref, acc, brick_v, brick_s, f1, f2, sem):
+def splat_kernel(points_ref, rhs_ref, inv_ref, ysend_ref, zsend_ref, csend_ref, acc, brick_v, brick_s, f1, f2, sem):
     sources = points_ref.shape[0] // 8
     brick_v[...] = points_ref[pl.ds(6, sources, stride=8), :].astype(I32)
     copy = pltpu.make_async_copy(brick_v, brick_s, sem)
@@ -366,13 +401,13 @@
                 f1[colour, zp, 1 : Y_DEV + 1] = y[colour]
                 f2[colour, zp + 1] = z[colour]
                 inv_ref[colour, zp] = 1.0 / (32.0 + 48.0 * d[colour])
-                yface_ref[0, colour, zp] = y[colour][0]
-                yface_ref[1, colour, zp] = y[colour][Y_DEV - 1]
+                ysend_ref[0, 16 + colour * HALF + zp] = y[colour][0]
+                ysend_ref[1, 16 + colour * HALF + zp] = y[colour][Y_DEV - 1]
         return 0
 
     lax.fori_loop(0, HALF // 2, planes, 0)
-    zface_ref[0] = acc[0:Y_DEV, 16:24, :]
-    zface_ref[1] = acc[(Z_DEV - 1) * Y_DEV :, 16:24, :]
+    zsend_ref[0, 16:32] = acc[0:Y_DEV, 16:24, :]
+    zsend_ref[1, 16:32] = acc[(Z_DEV - 1) * Y_DEV :, 16:24, :]
     for colour in range(2):
         f2[colour, 0] = swap_halves(jnp.where(low, f2[colour, HALF], 0.0))
         f2[colour, HALF + 1] = swap_halves(jnp.where(low, 0.0, f2[colour, 1]))
@@ -385,106 +420,172 @@
         return 0
 
     lax.fori_loop(0, HALF, finish, 0)
-
-
-def relax_kernel(rhs_in, inv_ref, start_ref, yface_ref, zface_ref, out_ref, v, edge, rhs, yin, zfin, face, send, recv, fsend, frecv):
+    ends = (0, Y_DEV - 1)
+    for s, y in enumerate(ends):
+        ysend_ref[s, 0:HALF] = rhs_ref[0, :, y]
+        ysend_ref[s, HALF : 2 * HALF] = inv_ref[0, :, y]
+        for t in range(2):
+            ysend_ref[s, 32 + t] = zsend_ref[t, 16 + y]
+    for t, zp in enumerate((0, HALF - 1)):
+        pack = pack_top if t == 1 else pack_bottom
+        for q, ref in enumerate((rhs_ref, inv_ref)):
+            zsend_ref[t, q * HALF : (q + 1) * HALF] = pack(ref[0, zp, :HALF], ref[0, zp, HALF:])
+        for s, y in enumerate(ends):
+            slope = f1[1, zp, y + 1]
+            zsend_ref[t, 32 + s] = slope
+            for q, tile in enumerate((rhs_ref[0, zp, y], inv_ref[0, zp, y], slope, zsend_ref[t, 16 + y])):
+                csend_ref[2 * t + s, q] = tile
+
+
+def relax_kernel(
+    rhs_in, inv_in, start_ref, ysend_ref, zsend_ref, csend_ref, out_ref,
+    v, edge, face, beside, red, red_inv, black, yin, zin, cin, send, recv, fsend, frecv,
+):
     grid = Grid()
+    grid.greet_neighbours()
+    w, end = WIDE, WIDE + Y_DEV
     versions = [start_ref.at[0], start_ref.at[1]] + [v.at[n] for n in range(2 * SWEEPS - 1)]
-
-    def clear(n, _):
-        grid.clear_outside(v.at[n], edge.at[n])
-        return 0
-
-    grid.greet_neighbours()
-    lax.fori_loop(0, 2 * SWEEPS - 1, clear, 0)
-    for d in FACES:
-        s = 0 if sum(d) == 1 else 1
-
-        @pl.when(jnp.logical_not(grid.exists((-d[0], -d[1]))))
-        def _():
-            if d[0] == 0:
-                yin[s] = jnp.zeros(yin.shape[1:], F32)
-            else:
-                zfin[s] = jnp.zeros(zfin.shape[1:], F32)
-
-    def update(step, zp, y, count):
-        zp, parity = (zp, zp) if isinstance(zp, int) else zp
+    plans = [
+        grid.halo(versions[n + 2], edge.at[n], face.at[n], beside.at[n // 2] if n % 2 == 0 else None)
+        for n in range(2 * SWEEPS - 2)
+    ]
+    for plan in plans:
+        grid.clear(landing(plan))
+    fields = []
+    for d in SIDES:
+        to = [(int(x == 1), int(x != 1)) for x in d]
+        if d[0] == 0:
+            fields.append((d, ysend_ref.at[to[1][0]], yin.at[to[1][1]]))
+        elif d[1] == 0:
+            fields.append((d, zsend_ref.at[to[0][0]], zin.at[to[0][1]]))
+        else:
+            fields.append((d, csend_ref.at[2 * to[0][0] + to[1][0]], cin.at[2 * to[0][1] + to[1][1]]))
+    grid.clear(landing(fields))
+    for zp in range(HALF):
+        red[zp + 1, 1 : Y_DEV + 1] = rhs_in[0, zp]
+        red_inv[zp + 1, 1 : Y_DEV + 1] = inv_in[0, zp]
+        black[zp] = rhs_in[1, zp]
+
+    def update(step, plane, y, count):
+        plane, parity = (plane, plane) if isinstance(plane, int) else plane
         same, opp, colour = versions[step], versions[step + 1], step % 2
-        outer = count == 1 or (isinstance(zp, int) and zp in (0, HALF - 1))
-        right = (rhs if outer else rhs_in)[colour, zp, y : y + count]
-        parity = (parity + y + colour) % 2
-        s1 = same[zp, y : y + count + 2] + same[zp + 2, y : y + count + 2]
-        o1 = opp[zp, y : y + count + 2] + opp[zp + 2, y : y + count + 2]
-        s0 = same[zp + 1, y : y + count + 2]
+        if colour == 0:
+            right, scale = red[plane - 1, y - 1 : y - 1 + count], red_inv[plane - 1, y - 1 : y - 1 + count]
+        else:
+            right, scale = black[plane - w, y - w : y - w + count], inv_in[1, plane - w, y - w : y - w + count]
+        s1 = same[plane - 1, y - 1 : y + count + 1] + same[plane + 1, y - 1 : y + count + 1]
+        o1 = opp[plane - 1, y - 1 : y + count + 1] + opp[plane + 1, y - 1 : y + count + 1]
+        s0 = same[plane, y - 1 : y + count + 1]
         around = s1[1:-1] + s0[:-2] + s0[2:]
         diagonal = s1[:-2] + s1[2:]
         across = 2.0 * around + (o1[:-2] + o1[2:])
         total = right + 2.0 * diagonal + across
-        other = neighbour(across, parity) if count == 1 else by_rows(across, parity, neighbour)
-        value = (total + other) * inv_ref[colour, zp, y : y + count]
-        if step < 2 * SWEEPS - 1:
-            versions[step + 2][zp + 1, y + 1 : y + 1 + count] = value
-        if step >= 2 * SWEEPS - 2:
-            out_ref[colour, zp, y : y + count] = value
-
-    def inner(step):
-        def planes(pair, _):
+        value = (total + by_rows(across, (parity + y + colour) % 2, neighbour)) * scale
+        if step == 2 * SWEEPS - 1:
+            out_ref[1, plane - w, y - w : y - w + count] = value
+        else:
+            versions[step + 2][plane, y : y + count] = value
+
+    def inside(step, first, planes, y, count):
+        def pair(i, _):
             for odd in range(2):
-                update(step, (pair * 2 + 1 + odd, 1 + odd), 1, Y_DEV - 2)
+                update(step, (i * 2 + first + odd, first + odd), y, count)
             return 0
 
-        lax.fori_loop(0, HALF // 2 - 1, planes, 0)
-
-    def outer(step):
-        for zp in (0, HALF - 1):
-            update(step, zp, 0, Y_DEV)
-        for zp in range(1, HALF - 1):
-            for y in (0, Y_DEV - 1):
-                update(step, zp, y, 1)
-
-    faces = []
-    for q, d in enumerate(FACES):
-        s = 0 if sum(d) == 1 else 1
-        src, dst = (yface_ref, yin) if d[0] == 0 else (zface_ref, zfin)
-        faces.append(
-            (d, pltpu.make_async_remote_copy(src.at[1 - s], dst.at[s], fsend.at[q], frecv.at[q], grid.device(d), MESH))
-        )
-    inner(0)
+        lax.fori_loop(0, planes // 2, pair, 0)
+
+    def red_inside(sweep):
+        inside(2 * sweep, w + 1, HALF - 2, w + 1, Y_DEV - 2)
+
+    def red_outside(sweep):
+        for plane in (w - 1, w, w + HALF - 1, w + HALF):
+            update(2 * sweep, plane, w - 1, Y_DEV + 2)
+        for plane in range(w + 1, w + HALF - 1):
+            for y in (w - 1, end - 1):
+                update(2 * sweep, plane, y, 2)
+
+    def black_outside(sweep):
+        for plane in (w, w + 1, w + HALF - 2, w + HALF - 1):
+            update(2 * sweep + 1, plane, w, Y_DEV)
+        for plane in range(w + 2, w + HALF - 2):
+            for y in (w, end - 2):
+                update(2 * sweep + 1, plane, y, 2)
+
+    def black_inside(sweep):
+        inside(2 * sweep + 1, w + 2, HALF - 4, w + 2, Y_DEV - 4)
+
+    red_inside(0)
     grid.await_neighbours()
-    grid.start(faces)
-    low = low_half((Y_DEV, *TILE))
-    for colour in range(2):
-        for zp in (0, HALF - 1):
-            rhs[colour, zp] = rhs_in[colour, zp]
-        for zp in range(1, HALF - 1):
-            for y in (0, Y_DEV - 1):
-                rhs[colour, zp, y] = rhs_in[colour, zp, y]
-    grid.take(faces)
-    for colour in range(2):
-        for zp in range(HALF):
-            rhs[colour, zp, 0] += 6.0 * yin[0, 1 - colour, zp]
-            rhs[colour, zp, Y_DEV - 1] -= 6.0 * yin[1, 1 - colour, zp]
-        below, above = zfin[0], zfin[1]
-        if colour == 1:
-            below, above = swap_halves(below), swap_halves(above)
-        rhs[colour, 0] += jnp.where(low, 6.0 * below, 0.0)
-        rhs[colour, HALF - 1] -= jnp.where(low, 0.0, 6.0 * above)
-
-    sent = [faces]
-    for step in range(2 * SWEEPS):
-        outer(step)
-        if step < 2 * SWEEPS - 1:
-            new = versions[step + 2]
-            pack_faces(new, face.at[step])
-            pairs = grid.halo(new, edge.at[step], face.at[step], send.at[step], recv.at[step])
+    pairs = grid.copies(fields, fsend, frecv)
+    grid.start(pairs)
+    sent = [pairs]
+    grid.take(pairs)
+
+    for tiles, q in ((red, 0), (red_inv, 1)):
+        for s, y in enumerate((0, Y_DEV + 1)):
+            tiles[1 : HALF + 1, y] = yin[s, q * HALF : (q + 1) * HALF]
+        sides = [
+            jnp.concatenate([zin[t, q * HALF : (q + 1) * HALF], cin[2 * t, q : q + 1], cin[2 * t + 1, q : q + 1]], axis=0)
+            for t in range(2)
+        ]
+        rim_planes(tiles, 1, 0, sides[0], sides[1])
+
+    def slopes(own, below, above):
+        return jnp.concatenate([under(own[HALF - 1 :], below), own, over(own[:1], above)], axis=0)
+
+    inner_y = [slopes(ysend_ref[s, 24:32], zin[0, 32 + s : 33 + s], zin[1, 32 + s : 33 + s]) for s in range(2)]
+    outer_y = [slopes(yin[s, 24:32], cin[s, 2:3], cin[2 + s, 2:3]) for s in range(2)]
+    red[:, 0] -= 6.0 * inner_y[0]
+    red[:, 1] += 6.0 * outer_y[0]
+    red[:, Y_DEV] -= 6.0 * outer_y[1]
+    red[:, Y_DEV + 1] += 6.0 * inner_y[1]
+    black[:, 0] += 6.0 * yin[0, 16:24]
+    black[:, Y_DEV - 1] -= 6.0 * yin[1, 16:24]
+
+    low = low_half((Y_DEV + 2, *TILE))
+    inner_z = [
+        jnp.concatenate([yin[0, 32 + t : 33 + t], zsend_ref[t, 16:32], yin[1, 32 + t : 33 + t]], axis=0) for t in range(2)
+    ]
+    outer_z = [
+        jnp.concatenate([cin[2 * t, 3:4], zin[t, 16:32], cin[2 * t + 1, 3:4]], axis=0) for t in range(2)
+    ]
+    red[0] -= jnp.where(low, 6.0 * swap_halves(inner_z[0]), 0.0)
+    red[1] += jnp.where(low, 6.0 * outer_z[0], 0.0)
+    red[HALF] -= jnp.where(low, 0.0, 6.0 * outer_z[1])
+    red[HALF + 1] += jnp.where(low, 0.0, 6.0 * swap_halves(inner_z[1]))
+    black[0] += jnp.where(low[1:-1], 6.0 * swap_halves(zin[0, 16:32]), 0.0)
+    black[HALF - 1] -= jnp.where(low[1:-1], 0.0, 6.0 * swap_halves(zin[1, 16:32]))
+
+    for sweep in range(SWEEPS):
+        final = sweep == SWEEPS - 1
+        news = (2 * sweep, 2 * sweep + 1)
+        flying = []
+
+        def launch(n):
+            pack_faces(versions[n + 2], face.at[n])
+            pairs = grid.copies(plans[n], send.at[n], recv.at[n])
             grid.start(pairs)
-            sent.append(pairs)
-        if step > 0:
-            inner(step)
-        if step < 2 * SWEEPS - 1:
-            grid.take(pairs)
-            rims(new, edge.at[step])
-
+            flying.append(pairs)
+
+        red_outside(sweep)
+        if not final:
+            launch(news[0])
+        black_outside(sweep)
+        if not final:
+            launch(news[1])
+        black_inside(sweep)
+        if not final:
+            red_inside(sweep + 1)
+            for n, pairs in zip(news, flying):
+                grid.take(pairs)
+                if n % 2 == 0:
+                    for s, y in enumerate((0, end)):
+                        versions[n + 2][w : w + HALF, y : y + w] = beside[n // 2, s]
+                rims(versions[n + 2], edge.at[n])
+            sent += flying
+
+    for zp in range(HALF):
+        out_ref[0, zp] = versions[2 * SWEEPS][zp + w, w:end]
     for pairs in sent:
         grid.sent(pairs)
 
@@ -523,7 +624,7 @@
 
 def shards(slot_brick, slot_count, point_cell, point_frac, point_normal, point_weight, guess):
     peers = point_cell.shape[1]
-    full = jax.ShapeDtypeStruct((2, HALF, Y_DEV, *TILE), F32)
+    full = jax.ShapeDtypeStruct((2, *FULL), F32)
     steps = 2 * SWEEPS - 1
 
     def last(x):
@@ -532,13 +633,13 @@
     args = (last(slot_brick), last(slot_count), last(point_cell), last(point_frac), last(point_normal), last(point_weight), guess)
     points, start = call(
         bin_kernel,
-        (jax.ShapeDtypeStruct((peers * 8, 128), F32), jax.ShapeDtypeStruct((2, *RIM), F32)),
+        (jax.ShapeDtypeStruct((peers * 8, 128), F32), jax.ShapeDtypeStruct((2, *rimmed(WIDE)), F32)),
         [pltpu.VMEM(a.shape, a.dtype) for a in args]
         + [
             pltpu.VMEM((peers * 8, 128), F32),
             pltpu.VMEM((2 * HALF * Y_DEV * 8, 128), F32),
-            pltpu.VMEM((2, *EDGE), F32),
-            pltpu.VMEM((2, 2, HALF, *TILE), F32),
+            pltpu.VMEM((2, *edge_shape(WIDE)), F32),
+            pltpu.VMEM((2, 2, WIDE, HALF, *TILE), F32),
             pltpu.SemaphoreType.DMA((7,)),
             pltpu.SemaphoreType.DMA,
             pltpu.SemaphoreType.DMA,
@@ -553,10 +654,11 @@
     outs = (
         full,
         full,
-        jax.ShapeDtypeStruct((2, 2, HALF, *TILE), F32),
-        jax.ShapeDtypeStruct((2, Y_DEV, *TILE), F32),
+        jax.ShapeDtypeStruct((2, 34, *TILE), F32),
+        jax.ShapeDtypeStruct((2, 34, *TILE), F32),
+        jax.ShapeDtypeStruct((4, 4, *TILE), F32),
     )
-    rhs, inv, yface, zface = call(
+    rhs, inv, ysend, zsend, csend = call(
         splat_kernel,
         outs,
         [
@@ -574,22 +676,26 @@
         relax_kernel,
         full,
         [
-            pltpu.VMEM((steps, *RIM), F32),
-            pltpu.VMEM((steps, *EDGE), F32),
-            pltpu.VMEM((2, HALF, Y_DEV, *TILE), F32),
-            pltpu.VMEM((2, 2, HALF, *TILE), F32),
-            pltpu.VMEM((2, Y_DEV, *TILE), F32),
-            pltpu.VMEM((steps, 2, HALF, *TILE), F32),
-            pltpu.SemaphoreType.DMA((steps, 8)),
-            pltpu.SemaphoreType.DMA((steps, 8)),
-            pltpu.SemaphoreType.DMA((4,)),
-            pltpu.SemaphoreType.DMA((4,)),
+            pltpu.VMEM((steps, *rimmed(WIDE)), F32),
+            pltpu.VMEM((steps - 1, *edge_shape(WIDE)), F32),
+            pltpu.VMEM((steps - 1, 2, WIDE, HALF, *TILE), F32),
+            pltpu.VMEM((SWEEPS - 1, 2, HALF, WIDE, *TILE), F32),
+            pltpu.VMEM(rimmed(1), F32),
+            pltpu.VMEM(rimmed(1), F32),
+            pltpu.VMEM(FULL, F32),
+            pltpu.VMEM((2, 34, *TILE), F32),
+            pltpu.VMEM((2, 34, *TILE), F32),
+            pltpu.VMEM((4, 4, *TILE), F32),
+            pltpu.SemaphoreType.DMA((steps - 1, 8)),
+            pltpu.SemaphoreType.DMA((steps - 1, 8)),
+            pltpu.SemaphoreType.DMA((8,)),
+            pltpu.SemaphoreType.DMA((8,)),
         ],
-        [VM] * 5,
+        [VM] * 6,
         32,
         collective_id=1,
         has_side_effects=True,
-    )(rhs, inv, start, yface, zface)
+    )(rhs, inv, start, ysend, zsend, csend)
     return call(interleave_kernel, jax.ShapeDtypeStruct((Z_DEV, Y_DEV, NX), F32), [], [VM], 16)(relaxed.reshape(-1, 128))
 
 

time: 59.8 us -> 52.6 us (0.88); the launches traced: 59.7 us -> 51.8 us
  Pallas kernels: 59.6 us -> 51.8 us
    pallas_call x1, Pallas kernels: 28.9 us -> 21 us  [shards(): call(relax_kernel, full, [pltpu.VMEM((steps, *rimmed(WIDE)), F32), pltpu....]
where the time goes in v3:
time: 52.6 us; the launch traced here: 51.8 us
  Pallas kernels  51.8 us (98%)
    pallas_call x1, Pallas kernels, shards(): call(relax_kernel, full, [pltpu.VMEM((steps, *rimmed(WIDE)), F32), pltpu....  21 us
    pallas_call x1, Pallas kernels, shards(): call(bin_kernel, (jax.ShapeDtypeStruct((peers * 8, 128), F32), jax.ShapeD...  20.3 us
    pallas_call x1, Pallas kernels, shards(): call(splat_kernel, outs, [pltpu.VMEM((Z_DEV * Y_DEV, 32, 128), F32), pltp...  8.99 us
    pallas_call x1, Pallas kernels, shards(): call(interleave_kernel, jax.ShapeDtypeStruct((Z_DEV, Y_DEV, NX), F32), []...  1.49 us

profile of v3, /device:TPU:7, one launch (start us, length us, event | category | flops | bytes accessed | tf_op | source)
XLA Modules:
  0.0 51.8 jit_solution(10857202233152280532)
XLA Ops:
  0.0 20.3 %shard_map.73 = (f32[1024,128]{1,0:T(8,128)S(1)}, f32[2,12,20,8,128]{4,3,2,1,0:T(8,128)S(1)}) custom-call(s32[2,128]{1,0:T(2,128)} %bitcast.24, s32[2,128]{1,0:T(2,128)} %bitcast.25, s32[2,64,128]{2,1,0:T(8,128)} %bitcast.21, f32[2,64,128]{2,1,0:T(8,128)} %bitcast.22, f32[2,3,64,128]{3,2,1,0:T(8,128)} %bitcast.20, f32[2,64,128]{2,1,0:T(8,128)} %bitcast.23, ...), custom_call_target="tpu_custom_call" | custom-call | tf_op jit(solution)/shard_map/pallas_call | solution.py:634
  20.3 9.0 %shard_map.74 = (f32[2,8,16,8,128]{4,3,2,1,0:T(8,128)S(1)}, f32[2,8,16,8,128]{4,3,2,1,0:T(8,128)S(1)}, f32[2,34,8,128]{3,2,1,0:T(8,128)S(1)}, f32[2,34,8,128]{3,2,1,0:T(8,128)S(1)}, f32[4,4,8,128]{3,2,1,0:T(8,128)S(1)}) custom-call(f32[1024,128]{1,0:T(8,128)S(1)} %get-tuple-element.12.points_ref), custom_call_target="tpu_custom_call" | custom-call | tf_op jit(solution)/shard_map/pallas_call | solution.py:661
  29.3 21.0 %shard_map.75 = f32[2,8,16,8,128]{4,3,2,1,0:T(8,128)S(1)} custom-call(f32[2,8,16,8,128]{4,3,2,1,0:T(8,128)S(1)} %get-tuple-element.13.rhs_in, f32[2,8,16,8,128]{4,3,2,1,0:T(8,128)S(1)} %get-tuple-element.14.inv_in, f32[2,12,20,8,128]{4,3,2,1,0:T(8,128)S(1)} %get-tuple-element.15.start_ref, f32[2,34,8,128]{3,2,1,0:T(8,128)S(1)} %get-tuple-element.16.ysend_ref, ...), custom_call_target="tpu_custom_call" | custom-call | tf_op jit(solution)/shard_map/pallas_call | solution.py:675
  50.3 1.5 %shard_map.76 = f32[16,16,1024]{2,1,0:T(8,128)} custom-call(f32[2048,128]{1,0:T(8,128)S(1)} %bitcast.19), custom_call_target="tpu_custom_call" | custom-call | tf_op jit(solution)/shard_map/pallas_call | solution.py:699

commit v4 on v3

--- a/solution.py
+++ b/solution.py
@@ -79,6 +79,7 @@
 
 SIDES = [(1, 1), (1, -1), (-1, 1), (-1, -1), (1, 0), (-1, 0), (0, 1), (0, -1)]
 WIDE = 2
+ROWS = 7
 FULL = (HALF, Y_DEV, *TILE)
 
 
@@ -241,14 +242,21 @@
     for plan in plans:
         grid.clear(landing(plan))
 
-    def peer(i):
-        return lax.rem(me + i + 1, peers)
-
-    def greet(i, _):
-        pl.semaphore_signal(barrier, inc=1, device_id=peer(i), device_id_type=LOGICAL)
-        return 0
-
-    lax.fori_loop(0, peers - 1, greet, 0)
+    sizes = (4, 4, 2, 4) if peers == 128 else (1, 1, grid.ns, grid.nr)
+    strides = [sizes[1] * sizes[2] * sizes[3], sizes[2] * sizes[3], sizes[3], 1]
+    shifted = [
+        [lax.rem(lax.rem(me // stride, size) + k, size) * stride for k in range(size)]
+        for stride, size in zip(strides, sizes)
+    ]
+    steps = [(z, x, c, y) for z in range(sizes[0]) for x in range(sizes[1]) for c in range(sizes[2]) for y in range(sizes[3])]
+    hops = {o: sum(min(k, size - k) for k, size in zip(o, sizes)) for o in steps}
+    order = sorted(steps[1:], key=lambda o: -hops[o])
+
+    def peer(o):
+        return sum(column[k] for column, k in zip(shifted, o))
+
+    for o in order:
+        pl.semaphore_signal(barrier, inc=1, device_id=peer(o), device_id_type=LOGICAL)
 
     loads[0].wait()
     deinterleave(guess_ref, split)
@@ -264,8 +272,8 @@
     live = jnp.concatenate([(point < count_ref[s : s + 1, :]).astype(F32) for s in range(S_PEER)], axis=0)
 
     def put(r, first, second, mask=None):
-        rows = jnp.concatenate([first, second], axis=0).astype(F32)
-        packed[pl.ds(r, peers, stride=8), :] = (rows if mask is None else rows * mask).T
+        both = jnp.concatenate([first, second], axis=0).astype(F32)
+        packed[pl.ds(r, peers, stride=8), :] = (both if mask is None else both * mask).T
 
     put(0, cell_ref[0], cell_ref[1])
     put(1, frac_ref[0], frac_ref[1])
@@ -273,28 +281,24 @@
         put(2 + ch, normal_ref[0, ch], normal_ref[1, ch], live)
     put(5, weight_ref[0], weight_ref[1], live)
     put(6, *[jnp.broadcast_to(brick_ref[s : s + 1, :], point.shape) for s in range(S_PEER)])
-    packed[pl.ds(7, peers, stride=8), :] = jnp.zeros((peers, 128), F32)
-
-    def tile(t):
-        return pl.ds(pl.multiple_of(t * 8, 8), 8)
+
+    def rows(t):
+        return pl.ds(pl.multiple_of(t * 8, 8), ROWS)
 
     pl.semaphore_wait(barrier, peers - 1)
 
-    def send_points(i, _):
-        t = peer(i)
-        pltpu.make_async_remote_copy(packed.at[tile(t)], points_ref.at[tile(me)], psend, precv, t, LOGICAL).start()
-        return 0
-
-    lax.fori_loop(0, peers - 1, send_points, 0)
+    for o in order:
+        t = peer(o)
+        pltpu.make_async_remote_copy(packed.at[rows(t)], points_ref.at[rows(me)], psend, precv, t, LOGICAL).start()
     halos = [grid.copies(plans[c], send.at[c], recv.at[c]) for c in range(2)]
     for colour in range(2):
         grid.start(halos[colour])
-    points_ref[tile(me), :] = packed[tile(me), :]
+    points_ref[rows(me), :] = packed[rows(me), :]
     for colour in range(2):
         grid.take(halos[colour])
         rims(v_ref.at[colour], edge.at[colour])
-    others = pl.ds(0, (peers - 1) * 8)
-    every = pltpu.make_async_remote_copy(packed.at[others], points_ref.at[others], psend, precv, peer(0), LOGICAL)
+    others = pl.ds(0, (peers - 1) * ROWS)
+    every = pltpu.make_async_remote_copy(packed.at[others], points_ref.at[others], psend, precv, peer(order[-1]), LOGICAL)
     every.wait_recv()
     every.wait_send()
     for colour in range(2):
@@ -370,7 +374,7 @@
                 acc[b] = acc[b] + (out[s * 64 : s * 64 + 32] + out[s * 64 + 32 : s * 64 + 64])
         return 0
 
-    lax.fori_loop(0, sources // 8, group, 0)
+    lax.fori_loop(0, sources // 8, group, 0, unroll=min(8, sources // 8))
 
     low = low_half((Y_DEV, *TILE))
 
@@ -401,8 +405,8 @@
                 f1[colour, zp, 1 : Y_DEV + 1] = y[colour]
                 f2[colour, zp + 1] = z[colour]
                 inv_ref[colour, zp] = 1.0 / (32.0 + 48.0 * d[colour])
-                ysend_ref[0, 16 + colour * HALF + zp] = y[colour][0]
-                ysend_ref[1, 16 + colour * HALF + zp] = y[colour][Y_DEV - 1]
+                ysend_ref[0, (26, 16)[colour] + zp] = y[colour][0]
+                ysend_ref[1, (26, 16)[colour] + zp] = y[colour][Y_DEV - 1]
         return 0
 
     lax.fori_loop(0, HALF // 2, planes, 0)
@@ -425,7 +429,7 @@
         ysend_ref[s, 0:HALF] = rhs_ref[0, :, y]
         ysend_ref[s, HALF : 2 * HALF] = inv_ref[0, :, y]
         for t in range(2):
-            ysend_ref[s, 32 + t] = zsend_ref[t, 16 + y]
+            ysend_ref[s, 24 + t] = zsend_ref[t, 16 + y]
     for t, zp in enumerate((0, HALF - 1)):
         pack = pack_top if t == 1 else pack_bottom
         for q, ref in enumerate((rhs_ref, inv_ref)):
@@ -439,7 +443,7 @@
 
 def relax_kernel(
     rhs_in, inv_in, start_ref, ysend_ref, zsend_ref, csend_ref, out_ref,
-    v, edge, face, beside, red, red_inv, black, yin, zin, cin, send, recv, fsend, frecv,
+    v, edge, face, beside, red, red_inv, black, yin, zin, cin, send, recv, fsend, frecv, lsend, lrecv,
 ):
     grid = Grid()
     grid.greet_neighbours()
@@ -451,16 +455,17 @@
     ]
     for plan in plans:
         grid.clear(landing(plan))
-    fields = []
+    fields, late = [], []
     for d in SIDES:
         to = [(int(x == 1), int(x != 1)) for x in d]
         if d[0] == 0:
-            fields.append((d, ysend_ref.at[to[1][0]], yin.at[to[1][1]]))
+            for plan, part in ((fields, pl.ds(0, 26)), (late, pl.ds(26, 8))):
+                plan.append((d, ysend_ref.at[to[1][0], part], yin.at[to[1][1], part]))
         elif d[1] == 0:
             fields.append((d, zsend_ref.at[to[0][0]], zin.at[to[0][1]]))
         else:
             fields.append((d, csend_ref.at[2 * to[0][0] + to[1][0]], cin.at[2 * to[0][1] + to[1][1]]))
-    grid.clear(landing(fields))
+    grid.clear(landing(fields) + landing(late))
     for zp in range(HALF):
         red[zp + 1, 1 : Y_DEV + 1] = rhs_in[0, zp]
         red_inv[zp + 1, 1 : Y_DEV + 1] = inv_in[0, zp]
@@ -497,19 +502,27 @@
     def red_inside(sweep):
         inside(2 * sweep, w + 1, HALF - 2, w + 1, Y_DEV - 2)
 
-    def red_outside(sweep):
-        for plane in (w - 1, w, w + HALF - 1, w + HALF):
+    def red_faces(sweep):
+        for plane in (w, w + HALF - 1):
             update(2 * sweep, plane, w - 1, Y_DEV + 2)
         for plane in range(w + 1, w + HALF - 1):
             for y in (w - 1, end - 1):
                 update(2 * sweep, plane, y, 2)
 
-    def black_outside(sweep):
-        for plane in (w, w + 1, w + HALF - 2, w + HALF - 1):
+    def red_ring(sweep):
+        for plane in (w - 1, w + HALF):
+            update(2 * sweep, plane, w - 1, Y_DEV + 2)
+
+    def black_faces(sweep):
+        for plane in (w, w + HALF - 1):
             update(2 * sweep + 1, plane, w, Y_DEV)
-        for plane in range(w + 2, w + HALF - 2):
+        for plane in range(w + 1, w + HALF - 1):
             for y in (w, end - 2):
                 update(2 * sweep + 1, plane, y, 2)
+
+    def black_second(sweep):
+        for plane in (w + 1, w + HALF - 2):
+            update(2 * sweep + 1, plane, w + 2, Y_DEV - 4)
 
     def black_inside(sweep):
         inside(2 * sweep + 1, w + 2, HALF - 4, w + 2, Y_DEV - 4)
@@ -517,8 +530,9 @@
     red_inside(0)
     grid.await_neighbours()
     pairs = grid.copies(fields, fsend, frecv)
-    grid.start(pairs)
-    sent = [pairs]
+    tail = grid.copies(late, lsend, lrecv)
+    grid.start(pairs + tail)
+    sent = [pairs, tail]
     grid.take(pairs)
 
     for tiles, q in ((red, 0), (red_inv, 1)):
@@ -533,18 +547,16 @@
     def slopes(own, below, above):
         return jnp.concatenate([under(own[HALF - 1 :], below), own, over(own[:1], above)], axis=0)
 
-    inner_y = [slopes(ysend_ref[s, 24:32], zin[0, 32 + s : 33 + s], zin[1, 32 + s : 33 + s]) for s in range(2)]
-    outer_y = [slopes(yin[s, 24:32], cin[s, 2:3], cin[2 + s, 2:3]) for s in range(2)]
+    inner_y = [slopes(ysend_ref[s, 16:24], zin[0, 32 + s : 33 + s], zin[1, 32 + s : 33 + s]) for s in range(2)]
+    outer_y = [slopes(yin[s, 16:24], cin[s, 2:3], cin[2 + s, 2:3]) for s in range(2)]
     red[:, 0] -= 6.0 * inner_y[0]
     red[:, 1] += 6.0 * outer_y[0]
     red[:, Y_DEV] -= 6.0 * outer_y[1]
     red[:, Y_DEV + 1] += 6.0 * inner_y[1]
-    black[:, 0] += 6.0 * yin[0, 16:24]
-    black[:, Y_DEV - 1] -= 6.0 * yin[1, 16:24]
 
     low = low_half((Y_DEV + 2, *TILE))
     inner_z = [
-        jnp.concatenate([yin[0, 32 + t : 33 + t], zsend_ref[t, 16:32], yin[1, 32 + t : 33 + t]], axis=0) for t in range(2)
+        jnp.concatenate([yin[0, 24 + t : 25 + t], zsend_ref[t, 16:32], yin[1, 24 + t : 25 + t]], axis=0) for t in range(2)
     ]
     outer_z = [
         jnp.concatenate([cin[2 * t, 3:4], zin[t, 16:32], cin[2 * t + 1, 3:4]], axis=0) for t in range(2)
@@ -561,18 +573,26 @@
         news = (2 * sweep, 2 * sweep + 1)
         flying = []
 
-        def launch(n):
+        def launch(n, between):
+            pairs = grid.copies(plans[n], send.at[n], recv.at[n])
+            between(sweep)
             pack_faces(versions[n + 2], face.at[n])
-            pairs = grid.copies(plans[n], send.at[n], recv.at[n])
             grid.start(pairs)
             flying.append(pairs)
 
-        red_outside(sweep)
+        red_faces(sweep)
         if not final:
-            launch(news[0])
-        black_outside(sweep)
+            launch(news[0], lambda _: None)
+        red_ring(sweep)
+        if sweep == 0:
+            grid.take(tail)
+            black[:, 0] += 6.0 * yin[0, 26:34]
+            black[:, Y_DEV - 1] -= 6.0 * yin[1, 26:34]
+        black_faces(sweep)
         if not final:
-            launch(news[1])
+            launch(news[1], black_second)
+        else:
+            black_second(sweep)
         black_inside(sweep)
         if not final:
             red_inside(sweep + 1)
@@ -690,6 +710,8 @@
             pltpu.SemaphoreType.DMA((steps - 1, 8)),
             pltpu.SemaphoreType.DMA((8,)),
             pltpu.SemaphoreType.DMA((8,)),
+            pltpu.SemaphoreType.DMA((2,)),
+            pltpu.SemaphoreType.DMA((2,)),
         ],
         [VM] * 6,
         32,

time: 52.6 us -> 47.6 us (0.905)
  Pallas kernels: 51.8 us -> 46.9 us
    pallas_call x1, Pallas kernels: 8.99 us -> 5.85 us  [shards(): call(splat_kernel, outs, [pltpu.VMEM((Z_DEV * Y_DEV, 32, 128), F32), pltp...]
    pallas_call x1, Pallas kernels: 20.3 us -> 18.4 us  [shards(): call(bin_kernel, (jax.ShapeDtypeStruct((peers * 8, 128), F32), jax.ShapeD...]
where the time goes in v4:
time: 47.6 us; the launch traced here: 46.9 us
  Pallas kernels  46.9 us (99%)
    pallas_call x1, Pallas kernels, shards(): call(relax_kernel, full, [pltpu.VMEM((steps, *rimmed(WIDE)), F32), pltpu....  21.1 us
    pallas_call x1, Pallas kernels, shards(): call(bin_kernel, (jax.ShapeDtypeStruct((peers * 8, 128), F32), jax.ShapeD...  18.4 us
    pallas_call x1, Pallas kernels, shards(): call(splat_kernel, outs, [pltpu.VMEM((Z_DEV * Y_DEV, 32, 128), F32), pltp...  5.85 us
    pallas_call x1, Pallas kernels, shards(): call(interleave_kernel, jax.ShapeDtypeStruct((Z_DEV, Y_DEV, NX), F32), []...  1.49 us

profile of v4, /device:TPU:7, one launch (start us, length us, event | category | flops | bytes accessed | tf_op | source)
XLA Modules:
  0.0 46.9 jit_solution(9433166541348809183)
XLA Ops:
  0.0 18.4 %shard_map.73 = (f32[1024,128]{1,0:T(8,128)S(1)}, f32[2,12,20,8,128]{4,3,2,1,0:T(8,128)S(1)}) custom-call(s32[2,128]{1,0:T(2,128)} %bitcast.24, s32[2,128]{1,0:T(2,128)} %bitcast.25, s32[2,64,128]{2,1,0:T(8,128)} %bitcast.21, f32[2,64,128]{2,1,0:T(8,128)} %bitcast.22, f32[2,3,64,128]{3,2,1,0:T(8,128)} %bitcast.20, f32[2,64,128]{2,1,0:T(8,128)} %bitcast.23, ...), custom_call_target="tpu_custom_call" | custom-call | tf_op jit(solution)/shard_map/pallas_call | solution.py:654
  18.4 5.9 %shard_map.74 = (f32[2,8,16,8,128]{4,3,2,1,0:T(8,128)S(1)}, f32[2,8,16,8,128]{4,3,2,1,0:T(8,128)S(1)}, f32[2,34,8,128]{3,2,1,0:T(8,128)S(1)}, f32[2,34,8,128]{3,2,1,0:T(8,128)S(1)}, f32[4,4,8,128]{3,2,1,0:T(8,128)S(1)}) custom-call(f32[1024,128]{1,0:T(8,128)S(1)} %get-tuple-element.12.points_ref), custom_call_target="tpu_custom_call" | custom-call | tf_op jit(solution)/shard_map/pallas_call | solution.py:681
  24.3 21.1 %shard_map.75 = f32[2,8,16,8,128]{4,3,2,1,0:T(8,128)S(1)} custom-call(f32[2,8,16,8,128]{4,3,2,1,0:T(8,128)S(1)} %get-tuple-element.13.rhs_in, f32[2,8,16,8,128]{4,3,2,1,0:T(8,128)S(1)} %get-tuple-element.14.inv_in, f32[2,12,20,8,128]{4,3,2,1,0:T(8,128)S(1)} %get-tuple-element.15.start_ref, f32[2,34,8,128]{3,2,1,0:T(8,128)S(1)} %get-tuple-element.16.ysend_ref, ...), custom_call_target="tpu_custom_call" | custom-call | tf_op jit(solution)/shard_map/pallas_call | solution.py:695
  45.4 1.5 %shard_map.76 = f32[16,16,1024]{2,1,0:T(8,128)} custom-call(f32[2048,128]{1,0:T(8,128)S(1)} %bitcast.19), custom_call_target="tpu_custom_call" | custom-call | tf_op jit(solution)/shard_map/pallas_call | solution.py:721

commit v5 on v4

--- a/solution.py
+++ b/solution.py
@@ -287,12 +287,17 @@
 
     pl.semaphore_wait(barrier, peers - 1)
 
-    for o in order:
+    halos = [grid.copies(plans[c], send.at[c], recv.at[c]) for c in range(2)]
+    for o in order[:32]:
         t = peer(o)
         pltpu.make_async_remote_copy(packed.at[rows(t)], points_ref.at[rows(me)], psend, precv, t, LOGICAL).start()
-    halos = [grid.copies(plans[c], send.at[c], recv.at[c]) for c in range(2)]
     for colour in range(2):
-        grid.start(halos[colour])
+        grid.start(halos[colour][:6])
+    for o in order[32:]:
+        t = peer(o)
+        pltpu.make_async_remote_copy(packed.at[rows(t)], points_ref.at[rows(me)], psend, precv, t, LOGICAL).start()
+    for colour in range(2):
+        grid.start(halos[colour][6:])
     points_ref[rows(me), :] = packed[rows(me), :]
     for colour in range(2):
         grid.take(halos[colour])
@@ -374,7 +379,7 @@
                 acc[b] = acc[b] + (out[s * 64 : s * 64 + 32] + out[s * 64 + 32 : s * 64 + 64])
         return 0
 
-    lax.fori_loop(0, sources // 8, group, 0, unroll=min(8, sources // 8))
+    lax.fori_loop(0, sources // 8, group, 0, unroll=min(16, sources // 8))
 
     low = low_half((Y_DEV, *TILE))
 
@@ -610,7 +615,8 @@
         grid.sent(pairs)
 
 
-def interleave_kernel(in_ref, out_ref):
+def interleave_kernel(in_ref, out_hbm, out_ref, sem):
+    copies = []
     col, row = iota((256, 256), 1), iota((256, 256), 0)
     place = (col == jnp.where(row < 128, 2 * row, 2 * row - 255)).astype(BF16)
     rows = Z_DEV * Y_DEV
@@ -625,18 +631,23 @@
         both = jnp.concatenate([jnp.where(even, red, black), jnp.where(even, black, red)], axis=1)
         high, low = parts(both)
         merged = jnp.dot(high, place, preferred_element_type=F32) + jnp.dot(low, place, preferred_element_type=F32)
-        out_ref[:, :, 256 * i : 256 * (i + 1)] = merged.reshape(Z_DEV, Y_DEV, 256)
+        out_ref[i] = merged.reshape(Z_DEV, Y_DEV, 256)
+        copy = pltpu.make_async_copy(out_ref.at[i], out_hbm.at[:, :, pl.ds(256 * i, 256)], sem.at[i])
+        copy.start()
+        copies.append(copy)
+    for copy in copies:
+        copy.wait()
 
 
 VM = pl.BlockSpec(memory_space=pltpu.VMEM)
 
 
-def call(kernel, outs, scratch, specs, limit, **params):
+def call(kernel, outs, scratch, specs, limit, out=VM, **params):
     return pl.pallas_call(
         kernel,
         out_shape=outs,
         in_specs=specs,
-        out_specs=jax.tree.map(lambda _: VM, outs),
+        out_specs=jax.tree.map(lambda _: out, outs),
         scratch_shapes=scratch,
         compiler_params=pltpu.CompilerParams(vmem_limit_bytes=limit << 20, **params),
     )
@@ -718,7 +729,14 @@
         collective_id=1,
         has_side_effects=True,
     )(rhs, inv, start, ysend, zsend, csend)
-    return call(interleave_kernel, jax.ShapeDtypeStruct((Z_DEV, Y_DEV, NX), F32), [], [VM], 16)(relaxed.reshape(-1, 128))
+    return call(
+        interleave_kernel,
+        jax.ShapeDtypeStruct((Z_DEV, Y_DEV, NX), F32),
+        [pltpu.VMEM((4, Z_DEV, Y_DEV, 256), F32), pltpu.SemaphoreType.DMA((4,))],
+        [VM],
+        16,
+        out=pl.BlockSpec(memory_space=pltpu.HBM),
+    )(relaxed.reshape(-1, 128))
 
 
 def solution(mesh):

time: 47.6 us -> 47.1 us (0.989)
  Pallas kernels: 46.9 us -> 46.3 us
where the time goes in v5:
time: 47.1 us; the launch traced here: 46.3 us
  Pallas kernels  46.3 us (98%)
    pallas_call x1, Pallas kernels, shards(): call(relax_kernel, full, [pltpu.VMEM((steps, *rimmed(WIDE)), F32), pltpu....  20.9 us
    pallas_call x1, Pallas kernels, shards(): call(bin_kernel, (jax.ShapeDtypeStruct((peers * 8, 128), F32), jax.ShapeD...  18.4 us
    pallas_call x1, Pallas kernels, shards(): call(splat_kernel, outs, [pltpu.VMEM((Z_DEV * Y_DEV, 32, 128), F32), pltp...  5.63 us
    pallas_call x1, Pallas kernels, shards(): call(interleave_kernel, jax.ShapeDtypeStruct((Z_DEV, Y_DEV, NX), F32), [p...  1.38 us

profile of v5, /device:TPU:7, one launch (start us, length us, event | category | flops | bytes accessed | tf_op | source)
XLA Modules:
  0.0 46.3 jit_solution(9427580630923417682)
XLA Ops:
  0.0 18.4 %shard_map.73 = (f32[1024,128]{1,0:T(8,128)S(1)}, f32[2,12,20,8,128]{4,3,2,1,0:T(8,128)S(1)}) custom-call(s32[2,128]{1,0:T(2,128)} %bitcast.24, s32[2,128]{1,0:T(2,128)} %bitcast.25, s32[2,64,128]{2,1,0:T(8,128)} %bitcast.21, f32[2,64,128]{2,1,0:T(8,128)} %bitcast.22, f32[2,3,64,128]{3,2,1,0:T(8,128)} %bitcast.20, f32[2,64,128]{2,1,0:T(8,128)} %bitcast.23, ...), custom_call_target="tpu_custom_call" | custom-call | tf_op jit(solution)/shard_map/pallas_call | solution.py:665
  18.4 5.6 %shard_map.74 = (f32[2,8,16,8,128]{4,3,2,1,0:T(8,128)S(1)}, f32[2,8,16,8,128]{4,3,2,1,0:T(8,128)S(1)}, f32[2,34,8,128]{3,2,1,0:T(8,128)S(1)}, f32[2,34,8,128]{3,2,1,0:T(8,128)S(1)}, f32[4,4,8,128]{3,2,1,0:T(8,128)S(1)}) custom-call(f32[1024,128]{1,0:T(8,128)S(1)} %get-tuple-element.12.points_ref), custom_call_target="tpu_custom_call" | custom-call | tf_op jit(solution)/shard_map/pallas_call | solution.py:692
  24.1 20.9 %shard_map.75 = f32[2,8,16,8,128]{4,3,2,1,0:T(8,128)S(1)} custom-call(f32[2,8,16,8,128]{4,3,2,1,0:T(8,128)S(1)} %get-tuple-element.13.rhs_in, f32[2,8,16,8,128]{4,3,2,1,0:T(8,128)S(1)} %get-tuple-element.14.inv_in, f32[2,12,20,8,128]{4,3,2,1,0:T(8,128)S(1)} %get-tuple-element.15.start_ref, f32[2,34,8,128]{3,2,1,0:T(8,128)S(1)} %get-tuple-element.16.ysend_ref, ...), custom_call_target="tpu_custom_call" | custom-call | tf_op jit(solution)/shard_map/pallas_call | solution.py:706
  45.0 1.4 %shard_map.76 = f32[16,16,1024]{2,1,0:T(8,128)} custom-call(f32[2048,128]{1,0:T(8,128)S(1)} %bitcast.19), custom_call_target="tpu_custom_call" | custom-call | tf_op jit(solution)/shard_map/pallas_call | solution.py:732
